TPU v7x, 32 devices: a whole 2x2x4 slice. The times are simulated.
32 devices in a mesh: rep: 2 (over y), fsdp: 8 (over z, x), tp: 2 (over core).
Axes of the slice: x: 2, y: 2, z: 4, core: 2. Of those that a mesh axis runs over, the one named last changes fastest.
Arguments:
- attn_global: float32 [24, 1024, 1024], P('rep', 'fsdp', 'tp'), may hold values from -6 to 6
- attn_momentum: float32 [24, 1024, 1024], P('rep', 'fsdp', 'tp'), may hold values from -6 to 6
- attn_inner: bfloat16 [2, 24, 1024, 1024], P('rep', None, 'fsdp', 'tp'), may hold values from -6 to 6
- norm_global: float32 [4, 1024], P('rep', 'tp'), may hold values from 0.5 to 1.5
- norm_momentum: float32 [4, 1024], P('rep', 'tp'), may hold values from -4 to 4
- norm_inner: bfloat16 [2, 4, 1024], P('rep', None, 'tp'), may hold values from 0.5 to 1.5
- emb_global: float32 [8, 2, 2008, 1024], P('fsdp', 'rep', None, 'tp'), may hold values from -6 to 6
- emb_momentum: float32 [8, 2, 2008, 1024], P('fsdp', 'rep', None, 'tp'), may hold values from -6 to 6
- emb_inner: bfloat16 [2, 32128, 1024], P('rep', 'fsdp', 'tp'), may hold values from -6 to 6
- basis: float32 [1024, 64], replicated, may hold values from -0.1875 to 0.1875
- touched: int32 [2, 8192], replicated, may hold values from 0 to 32127
Outputs:
- new_attn_global: float32 [24, 1024, 1024], P('rep', 'fsdp', 'tp')
- new_attn_momentum: float32 [24, 1024, 1024], P('rep', 'fsdp', 'tp')
- attn_weights: float32 [24, 1024, 1024], P(None, 'fsdp', 'tp')
- new_norm_global: float32 [4, 1024], P('rep', 'tp')
- new_norm_momentum: float32 [4, 1024], P('rep', 'tp')
- norm_weights: float32 [4, 1024], P(None, 'tp')
- new_emb_global: float32 [8, 2, 2008, 1024], P('fsdp', 'rep', None, 'tp')
- new_emb_momentum: float32 [8, 2, 2008, 1024], P('fsdp', 'rep', None, 'tp')
- emb_weights: float32 [32128, 1024], P('fsdp', 'tp')
All inputs are finite; a program needn't handle non-finite values.
Results may differ from a plain program's by a relative error of at most 0.0003.
Values sent between devices are 32-bit elements; how exact they have to be, the bound alone decides.
A program may use at most 128 MiB of HBM per device.

v0:
```python
import jax
import jax.numpy as jnp
from jax import lax
from jax.sharding import PartitionSpec as P

OUTER_RATE = 0.7
MOMENTUM = 0.9


def nesterov(global_part, momentum_part, outer_grad):
    fresh_momentum = MOMENTUM * momentum_part + outer_grad
    fresh_global = global_part - OUTER_RATE * (outer_grad + MOMENTUM * fresh_momentum)
    return (fresh_global, fresh_momentum)


def per_device(
    attn_global,
    attn_momentum,
    attn_inner,
    norm_global,
    norm_momentum,
    norm_inner,
    emb_global,
    emb_momentum,
    emb_inner,
    basis,
    touched,
):
    groups = lax.axis_size("rep") * 1.0
    rep_index = lax.axis_index("rep")
    attn_terms = attn_inner[0].astype(jnp.float32)
    norm_terms = norm_inner[0].astype(jnp.float32)
    attn_total, norm_total = lax.psum((attn_terms, norm_terms), "rep")
    attn_owned = attn_global.shape[0]
    norm_owned = norm_global.shape[0]
    attn_summed = lax.dynamic_slice_in_dim(attn_total, rep_index * attn_owned, attn_owned, 0)
    norm_summed = lax.dynamic_slice_in_dim(norm_total, rep_index * norm_owned, norm_owned, 0)
    new_attn_global, new_attn_momentum = nesterov(
        attn_global, attn_momentum, attn_global - attn_summed / groups
    )
    new_norm_global, new_norm_momentum = nesterov(
        norm_global, norm_momentum, norm_global - norm_summed / groups
    )
    block_rows = emb_inner.shape[1]
    half_rows = emb_global.shape[2]
    half_width = emb_global.shape[3]
    row_start = lax.axis_index("fsdp") * block_rows
    half_start = rep_index * half_rows
    positions = row_start + jnp.arange(block_rows, dtype=jnp.int32)
    matches = touched[:, :, None] == positions[None, None, :]
    touched_masks = jnp.any(matches, axis=1).astype(jnp.float32)
    counts = jnp.sum(touched_masks, axis=0)
    own_mask = lax.dynamic_index_in_dim(touched_masks, rep_index, 0, keepdims=False)
    half_counts = lax.dynamic_slice_in_dim(counts, half_start, half_rows, 0)
    basis_half = lax.dynamic_slice_in_dim(basis, lax.axis_index("tp") * half_width, half_width, 0)
    own_rows = emb_global[0, 0]
    own_momentum = emb_momentum[0, 0]
    global_coeff = jnp.dot(
        own_rows, basis_half, precision=lax.Precision.HIGHEST, preferred_element_type=jnp.float32
    )
    placed_global = lax.dynamic_update_slice_in_dim(
        jnp.zeros((block_rows, basis.shape[1]), jnp.float32),
        half_counts[:, None] * global_coeff,
        half_start,
        0,
    )
    inner_coeff = jnp.dot(
        emb_inner[0].astype(jnp.float32),
        basis_half,
        precision=lax.Precision.HIGHEST,
        preferred_element_type=jnp.float32,
    )
    coeff_term = placed_global - own_mask[:, None] * inner_coeff
    coeff_total = lax.psum(coeff_term.reshape(-1), ("rep", "tp")).reshape(coeff_term.shape)
    coeff_sum = lax.dynamic_slice_in_dim(coeff_total, half_start, half_rows, 0)
    emb_grad = (
        jnp.dot(
            coeff_sum,
            basis_half.T,
            precision=lax.Precision.HIGHEST,
            preferred_element_type=jnp.float32,
        )
        / groups
    )
    fresh_rows, fresh_momentum = nesterov(own_rows, own_momentum, emb_grad)
    new_emb_global = fresh_rows.reshape(emb_global.shape)
    new_emb_momentum = fresh_momentum.reshape(emb_momentum.shape)
    attn_weights, norm_weights, emb_halves = (
        lax.all_gather(new_attn_global, "rep", axis=0, tiled=True),
        lax.all_gather(new_norm_global, "rep", axis=0, tiled=True),
        lax.all_gather(new_emb_global, "rep", axis=1, tiled=True),
    )
    emb_weights = emb_halves.reshape(block_rows, half_width)
    return (
        new_attn_global,
        new_attn_momentum,
        attn_weights,
        new_norm_global,
        new_norm_momentum,
        norm_weights,
        new_emb_global,
        new_emb_momentum,
        emb_weights,
    )


def solution(mesh):
    placed = (
        P("rep", "fsdp", "tp"),
        P("rep", "fsdp", "tp"),
        P("rep", None, "fsdp", "tp"),
        P("rep", "tp"),
        P("rep", "tp"),
        P("rep", None, "tp"),
        P("fsdp", "rep", None, "tp"),
        P("fsdp", "rep", None, "tp"),
        P("rep", "fsdp", "tp"),
        P(),
        P(),
    )
    return jax.shard_map(
        per_device,
        mesh=mesh,
        in_specs=placed,
        out_specs=(
            P("rep", "fsdp", "tp"),
            P("rep", "fsdp", "tp"),
            P(None, "fsdp", "tp"),
            P("rep", "tp"),
            P("rep", "tp"),
            P(None, "tp"),
            P("fsdp", "rep", None, "tp"),
            P("fsdp", "rep", None, "tp"),
            P("fsdp", "tp"),
        ),
        check_vma=False,
    )
```

profile of v0, /device:TPU:0, one launch (start us, length us, event | category | flops | bytes accessed | tf_op | source)
XLA Modules:
  0.0 462.5 jit_solution(2869069424929339542)
XLA Ops:
  7.2 0.0 copy-start
  7.2 0.0 all-reduce.5.cloned.1.call-start
  7.3 42.0 %compare_reduce_fusion = pred[2,4016]{1,0:T(4,128)(4,1)S(1)} fusion(s32[2,8192]{1,0:T(2,128)} %param.21, s32[4016]{0:T(1024)S(1)} %iota_add_fusion), kind=kLoop, calls=%fused_computation | loop fusion | flops 131588256 | bytes 89632 | tf_op jit(solution)/shard_map/reduce_or | solution.py:51
  49.3 0.1 dynamic_slice.21
  49.4 0.0 copy-done
  49.4 5.9 %fusion.9 = f32[2008,64]{0,1:T(8,128)S(1)} fusion(f32[1,1,2008,512]{3,2,1,0:T(8,128)} %param.17, f32[2008]{0:T(1024)S(1)} %dynamic_slice.21, f32[1024,64]{0,1:T(8,128)S(1)} %copy-done, s32[]{:T(128)S(6)} %select_n.21), kind=kOutput, calls=%fused_computation.15 | convolution fusion | flops 789706240 | bytes 4765700 | tf_op jit(solution)/shard_map/dot_general | solution.py:58
  55.3 0.1 broadcast_in_dim.2
  55.3 0.8 dynamic_update_slice.3
  56.2 6.7 %fusion.1 = f32[4016,64]{0,1:T(8,128)} fusion(f32[4016,64]{0,1:T(8,128)S(1)} %dynamic_update_slice.3, bf16[1,4016,512]{2,1,0:T(8,128)(2,1)} %param.19, f32[4016]{0:T(1024)S(1)} %bitcast.35, f32[1024,64]{0,1:T(8,128)S(1)} %copy-done, s32[]{:T(128)S(6)} %select_n.21), kind=kOutput, calls=%fused_computation.3 | convolution fusion | flops 1579669504 | bytes 6336516 | tf_op jit(solution)/shard_map/dot_general | solution.py:67
  62.9 0.0 all-reduce.5.cloned.1.call-update
  62.9 0.0 all-reduce.3.cloned.1.call-start
  63.0 5.5 %bitcast_convert_fusion = f32[24,128,512]{2,1,0:T(8,128)} fusion(bf16[1,24,128,512]{3,2,1,0:T(8,128)(2,1)} %param.13), kind=kLoop, calls=%fused_computation.10 | loop fusion | flops 1572864 | bytes 9437184 | tf_op jit(solution)/shard_map/convert_element_type | solution.py:31
  68.4 0.0 all-reduce.3.cloned.1.call-update
  68.4 0.0 all-gather.7.cloned.1.call-start
  68.5 33.9 %all-reduce.5.cloned.1.call-done = f32[4016,64]{0,1:T(8,128)} async-done(((f32[4016,64]{0,1:T(8,128)}), f32[4016,64]{0,1:T(8,128)}) %all-reduce.5.cloned.1.call-update) | async-done | bytes 1028112 | tf_op jit(solution)/shard_map/psum | solution.py:74
  102.4 9.7 %fusion.5 = (f32[1,1,2008,512]{3,2,1,0:T(8,128)}, f32[2008,512]{1,0:T(8,128)}) fusion(f32[1,1,2008,512]{3,2,1,0:T(8,128)} %param.18, f32[1,1,2008,512]{3,2,1,0:T(8,128)} %param.17, f32[1024,64]{0,1:T(8,128)S(1)} %copy-done, s32[]{:T(128)S(6)} %select_n.21, f32[4016,64]{0,1:T(8,128)} %all-reduce.5.cloned.1.call-done, s32[]{:T(128)S(6)} %select_n.20), kind=kOutput, calls=%fused_computation.9 | convolution fusion | flops 796774400 | bytes 17104904 | tf_op jit(solution)/shard_map/dot_general | solution.py:77
  112.1 0.0 copy-start.3
  112.1 0.0 all-gather.7.cloned.1.call-update
  112.1 0.0 all-gather.5.cloned.1.call-start
  112.1 0.0 copy-start.5
  112.2 0.0 copy-start.6
  112.2 0.0 copy-start.7
  112.2 147.0 %all-reduce.3.cloned.1.call-done = f32[24,128,512]{2,1,0:T(8,128)} async-done(((f32[24,128,512]{2,1,0:T(8,128)}), f32[24,128,512]{2,1,0:T(8,128)}) %all-reduce.3.cloned.1.call-update) | async-done | bytes 6291472 | tf_op jit(solution)/shard_map/psum | solution.py:33
  259.1 0.0 copy-done.3
  259.2 6.8 %multiply_subtract_fusion = (f32[12,128,512]{2,1,0:T(8,128)}, f32[12,128,512]{2,1,0:T(8,128)}) fusion(f32[12,128,512]{2,1,0:T(8,128)S(1)} %copy-done.3, f32[24,128,512]{2,1,0:T(8,128)} %all-reduce.3.cloned.1.call-done, s32[]{:T(128)S(6)} %select_n.18, f32[12,128,512]{2,1,0:T(8,128)} %param.12), kind=kLoop, calls=%fused_computation.11 | loop fusion | flops 6291456 | bytes 15728644 | tf_op jit(solution)/shard_map/sub | solution.py:12
  266.0 0.0 all-gather.5.cloned.1.call-update
  266.0 0.0 copy-done.5
  266.0 5.0 %psum.22 = f32[4,512]{1,0:T(4,128)S(1)} all-reduce(f32[4,512]{1,0:T(4,128)S(1)} %bitcast_convert_fusion.1), channel_id=1, replica_groups=mesh['rep'=2,'fsdp'=8,'tp'=2] {'rep'}, use_global_device_ids=true, to_apply=%region_1.0 | all-reduce | flops 2048 | bytes 16384 | tf_op jit(solution)/shard_map/psum | solution.py:33
  271.0 0.0 copy-done.6
  271.0 0.0 copy-done.7
  271.1 0.6 multiply_subtract_fusion.2
  271.7 0.0 copy-start.4
  271.7 4.3 all-gather.1
  276.0 0.6 reshape.58
  276.6 86.9 %all-gather.7.cloned.1.call-done = f32[4016,512]{1,0:T(8,128)} async-done(((f32[2008,512]{1,0:T(8,128)}), f32[4016,512]{1,0:T(8,128)}) %all-gather.7.cloned.1.call-update) | async-done | bytes 8224784 | tf_op jit(solution)/shard_map/all_gather | solution.py:91
  363.5 82.4 %all-gather.5.cloned.1.call-done = f32[24,128,512]{2,1,0:T(8,128)} async-done(((f32[12,128,512]{2,1,0:T(8,128)}), f32[24,128,512]{2,1,0:T(8,128)}) %all-gather.5.cloned.1.call-update) | async-done | bytes 6291472 | tf_op jit(solution)/shard_map/all_gather | solution.py:89
  445.9 0.0 copy-start.2
  445.9 6.7 %copy.25 = f32[24,128,512]{2,1,0:T(8,128)} copy(f32[24,128,512]{2,1,0:T(8,128)} %all-gather.5.cloned.1.call-done) | data formatting | bytes 12582912
  452.6 0.0 copy-done.4
  452.6 0.0 copy-done.2
  452.6 0.0 copy-start.1
  452.6 3.3 copy.26
  456.0 0.0 copy-done.1
  (5 shorter events, 0.1 us)
Async XLA Ops:
  7.2 42.2 %copy-start = (f32[1024,64]{0,1:T(8,128)S(1)}, f32[1024,64]{0,1:T(8,128)}, u32[]{:S(2)}) copy-start(f32[1024,64]{0,1:T(8,128)} %param.20) | copy-start | bytes 786436
  7.2 95.2 %all-reduce.5.cloned.1.call-start = ((), (), s32[]{:S(2)}) async-start(), calls=%async_computation.2 | async-start | bytes 2097152 | tf_op jit(solution)/shard_map/psum | solution.py:74
  62.9 196.2 %all-reduce.3.cloned.1.call-start = ((), (), s32[]{:S(2)}) async-start(), calls=%async_computation | async-start | bytes 12582912 | tf_op jit(solution)/shard_map/psum | solution.py:33
  68.4 295.1 %all-gather.7.cloned.1.call-start = ((), (), s32[]{:S(2)}) async-start(), calls=%async_computation.3 | async-start | bytes 12337152 | tf_op jit(solution)/shard_map/all_gather | solution.py:91
  112.1 147.1 %copy-start.3 = (f32[12,128,512]{2,1,0:T(8,128)S(1)}, f32[12,128,512]{2,1,0:T(8,128)}, u32[]{:S(2)}) copy-start(f32[12,128,512]{2,1,0:T(8,128)} %param.11) | copy-start | bytes 9437188
  112.1 333.8 %all-gather.5.cloned.1.call-start = ((), (), s32[]{:S(2)}) async-start(), calls=%async_computation.1 | async-start | bytes 9437184 | tf_op jit(solution)/shard_map/all_gather | solution.py:89
  112.1 153.9 %copy-start.5 = (bf16[1,4,512]{2,1,0:T(4,128)(2,1)S(1)}, bf16[1,4,512]{2,1,0:T(4,128)(2,1)}, u32[]{:S(2)}) copy-start(bf16[1,4,512]{2,1,0:T(4,128)(2,1)} %param.16) | copy-start | bytes 12292
  112.2 158.9 %copy-start.6 = (f32[2,512]{1,0:T(2,128)S(1)}, f32[2,512]{1,0:T(2,128)}, u32[]{:S(2)}) copy-start(f32[2,512]{1,0:T(2,128)} %param.14) | copy-start | bytes 12292
  112.2 158.9 %copy-start.7 = (f32[2,512]{1,0:T(2,128)S(1)}, f32[2,512]{1,0:T(2,128)}, u32[]{:S(2)}) copy-start(f32[2,512]{1,0:T(2,128)} %param.15) | copy-start | bytes 12292
  271.7 181.0 %copy-start.4 = (f32[2,512]{1,0:T(2,128)}, f32[2,512]{1,0:T(2,128)S(1)}, u32[]{:S(2)}) copy-start(f32[2,512]{1,0:T(2,128)S(1)} %get-tuple-element.27) | copy-start | bytes 12292
  445.9 6.7 %copy-start.2 = (f32[4016,512]{1,0:T(8,128)S(1)}, f32[4016,512]{1,0:T(8,128)}, u32[]{:S(2)}) copy-start(f32[4016,512]{1,0:T(8,128)} %all-gather.7.cloned.1.call-done) | copy-start | bytes 24674308
  452.6 3.3 copy-start.1
Sparse Core Ops, SparseCore 0:
  63.0 39.2 all-reduce.4
  105.5 153.5 all-reduce.2
  261.3 102.2 all-gather.6
  365.5 80.3 all-gather.4
where the time goes:
time: 463 us
  waiting for transfers between devices  350 us (76%)
  other arithmetic  54.9 us (12%)
  matrix products  22.2 us (5%)
  between operations  13.9 us (3%)
  local copies, waits for them, and re-layouts  11.7 us (3%)
  blocking collectives  9.34 us (2%)
    psum x1, waiting for transfers between devices, per_device(): attn_total, norm_total = lax.psum((attn_terms, norm_terms), 'rep')  147 us
    all_gather x1, waiting for transfers between devices, per_device(): lax.all_gather(new_emb_global, 'rep', axis=1, tiled=True)  86.9 us
    all_gather x1, waiting for transfers between devices, per_device(): lax.all_gather(new_attn_global, 'rep', axis=0, tiled=True)  82.4 us
    reduce_or x1, other arithmetic, per_device(): touched_masks = jnp.any(matches, axis=1).astype(jnp.float32)  42 us
    psum x1, waiting for transfers between devices, per_device(): lax.psum(coeff_term.reshape(-1), ('rep', 'tp')).reshape(coeff_term.shape)  33.9 us
    unnamed x19, local copies, waits for them, and re-layouts  10.7 us
    dot_general x1, matrix products, per_device(): jnp.dot(coeff_sum, basis_half.T, precision=lax.Precision.HIGHEST, preferr...  9.69 us
  transfers between devices with their start and end apart: 4, of which 4 were waited for; matrix products, arithmetic and copies ran while one was open for 5% of the time, Pallas kernels for 0%

commit v1 on v0

v1 whole, which is shorter than its diff:
```python
import jax
import jax.numpy as jnp
from jax import lax
from jax.sharding import PartitionSpec as P

OUTER_RATE = 0.7
MOMENTUM = 0.9
SWAP = ((0, 1), (1, 0))
ATTN_CHUNKS = 2
EMB_CHUNKS = 4
LOW = 256


def nesterov(global_part, momentum_part, outer_grad):
    fresh_momentum = MOMENTUM * momentum_part + outer_grad
    fresh_global = global_part - OUTER_RATE * (outer_grad + MOMENTUM * fresh_momentum)
    return (fresh_global, fresh_momentum)


def cuts(total, parts, unit):
    units = -(-total // unit)
    bounds = [min(total, unit * (units * i // parts)) for i in range(parts + 1)]
    return [(a, b) for a, b in zip(bounds[:-1], bounds[1:]) if b > a]


def swap(x, axis):
    return lax.ppermute(x, axis, SWAP)


def row_masks(touched, row_start, block_rows):
    high_count = -(-block_rows // LOW)
    local = touched - row_start
    high = jnp.floor_divide(local, LOW)
    low = local - high * LOW
    high_hot = (high[:, None, :] == jnp.arange(high_count, dtype=jnp.int32)[None, :, None]).astype(jnp.bfloat16)
    low_hot = (low[:, None, :] == jnp.arange(LOW, dtype=jnp.int32)[None, :, None]).astype(jnp.bfloat16)
    times = jnp.einsum("rht,rlt->rhl", high_hot, low_hot, preferred_element_type=jnp.float32)
    masks = (times > 0.5).astype(jnp.float32)
    return masks.reshape(touched.shape[0], high_count * LOW)[:, :block_rows]


def coeff_of(rows, basis_half):
    return lax.dot_general(
        basis_half,
        rows,
        (((0,), (1,)), ((), ())),
        precision=lax.Precision.HIGHEST,
        preferred_element_type=jnp.float32,
    )


def per_device(
    attn_global,
    attn_momentum,
    attn_inner,
    norm_global,
    norm_momentum,
    norm_inner,
    emb_global,
    emb_momentum,
    emb_inner,
    basis,
    touched,
):
    groups = lax.axis_size("rep") * 1.0
    rep_index = lax.axis_index("rep")
    tp_index = lax.axis_index("tp")
    other = 1 - rep_index
    attn_owned = attn_global.shape[0]
    norm_owned = norm_global.shape[0]
    block_rows = emb_inner.shape[1]
    half_rows = emb_global.shape[2]
    half_width = emb_global.shape[3]
    rank = basis.shape[1]

    attn_cuts = cuts(attn_owned, ATTN_CHUNKS, 1)
    arrived = []
    for a, b in attn_cuts:
        part = lax.dynamic_slice_in_dim(attn_inner[0], other * attn_owned + a, b - a, 0)
        arrived.append(swap(part.astype(jnp.float32) / groups, "rep"))
    norm_part = lax.dynamic_slice_in_dim(norm_inner[0], other * norm_owned, norm_owned, 0)
    norm_arrived = swap(norm_part.astype(jnp.float32) / groups, "rep")

    half_start = rep_index * half_rows
    other_start = other * half_rows
    masks = row_masks(touched, lax.axis_index("fsdp") * block_rows, block_rows)
    counts = jnp.sum(masks, axis=0)
    own_mask = lax.dynamic_index_in_dim(masks, rep_index, 0, keepdims=False)
    half_counts = lax.dynamic_slice_in_dim(counts, half_start, half_rows, 0)
    basis_half = lax.dynamic_slice_in_dim(basis, tp_index * half_width, half_width, 0)
    own_rows = emb_global[0, 0]
    own_momentum = emb_momentum[0, 0]
    global_coeff = half_counts[None, :] * coeff_of(own_rows, basis_half)
    inner_coeff = own_mask[None, :] * coeff_of(emb_inner[0].astype(jnp.float32), basis_half)
    own_term = global_coeff - lax.dynamic_slice_in_dim(inner_coeff, half_start, half_rows, 1)
    other_term = -lax.dynamic_slice_in_dim(inner_coeff, other_start, half_rows, 1)
    terms = jnp.stack((own_term, other_term))
    half_rank = rank // 2
    kept = lax.dynamic_slice_in_dim(terms, tp_index * half_rank, half_rank, 1)
    given = lax.dynamic_slice_in_dim(terms, (1 - tp_index) * half_rank, half_rank, 1)
    summed = kept + swap(given, "tp")
    coeff_mine = summed[0] + swap(summed[1], "rep")
    coeff_theirs = swap(coeff_mine, "tp")
    first = tp_index == 0
    coeff_sum = jnp.concatenate(
        (
            jnp.where(first, coeff_mine, coeff_theirs),
            jnp.where(first, coeff_theirs, coeff_mine),
        ),
        axis=0,
    )
    emb_grad = (
        lax.dot_general(
            coeff_sum,
            basis_half,
            (((0,), (1,)), ((), ())),
            precision=lax.Precision.HIGHEST,
            preferred_element_type=jnp.float32,
        )
        / groups
    )
    fresh_rows, fresh_momentum = nesterov(own_rows, own_momentum, emb_grad)

    fresh_global = []
    fresh_attn_momentum = []
    returned = []
    for (a, b), got in zip(attn_cuts, arrived):
        part = lax.dynamic_slice_in_dim(attn_inner[0], rep_index * attn_owned + a, b - a, 0)
        mean = part.astype(jnp.float32) / groups + got
        now, moved = nesterov(attn_global[a:b], attn_momentum[a:b], attn_global[a:b] - mean)
        fresh_global.append(now)
        fresh_attn_momentum.append(moved)
        returned.append(swap(now, "rep"))
    new_attn_global = jnp.concatenate(fresh_global, axis=0)
    new_attn_momentum = jnp.concatenate(fresh_attn_momentum, axis=0)
    attn_weights = jnp.zeros((2 * attn_owned,) + attn_global.shape[1:], jnp.float32)
    attn_weights = lax.dynamic_update_slice_in_dim(attn_weights, new_attn_global, rep_index * attn_owned, 0)
    for (a, b), got in zip(attn_cuts, returned):
        attn_weights = lax.dynamic_update_slice_in_dim(attn_weights, got, other * attn_owned + a, 0)

    norm_own = lax.dynamic_slice_in_dim(norm_inner[0], rep_index * norm_owned, norm_owned, 0)
    norm_mean = norm_own.astype(jnp.float32) / groups + norm_arrived
    new_norm_global, new_norm_momentum = nesterov(norm_global, norm_momentum, norm_global - norm_mean)
    norm_weights = jnp.zeros((2 * norm_owned,) + norm_global.shape[1:], jnp.float32)
    norm_weights = lax.dynamic_update_slice_in_dim(norm_weights, new_norm_global, rep_index * norm_owned, 0)
    norm_weights = lax.dynamic_update_slice_in_dim(
        norm_weights, swap(new_norm_global, "rep"), other * norm_owned, 0
    )

    emb_weights = jnp.zeros((block_rows, half_width), jnp.float32)
    emb_weights = lax.dynamic_update_slice_in_dim(emb_weights, fresh_rows, half_start, 0)
    for a, b in cuts(half_rows, EMB_CHUNKS, 8):
        got = swap(fresh_rows[a:b], "rep")
        emb_weights = lax.dynamic_update_slice_in_dim(emb_weights, got, other_start + a, 0)

    return (
        new_attn_global,
        new_attn_momentum,
        attn_weights,
        new_norm_global,
        new_norm_momentum,
        norm_weights,
        fresh_rows.reshape(emb_global.shape),
        fresh_momentum.reshape(emb_momentum.shape),
        emb_weights,
    )


def solution(mesh):
    placed = (
        P("rep", "fsdp", "tp"),
        P("rep", "fsdp", "tp"),
        P("rep", None, "fsdp", "tp"),
        P("rep", "tp"),
        P("rep", "tp"),
        P("rep", None, "tp"),
        P("fsdp", "rep", None, "tp"),
        P("fsdp", "rep", None, "tp"),
        P("rep", "fsdp", "tp"),
        P(),
        P(),
    )
    return jax.shard_map(
        per_device,
        mesh=mesh,
        in_specs=placed,
        out_specs=(
            P("rep", "fsdp", "tp"),
            P("rep", "fsdp", "tp"),
            P(None, "fsdp", "tp"),
            P("rep", "tp"),
            P("rep", "tp"),
            P(None, "tp"),
            P("fsdp", "rep", None, "tp"),
            P("fsdp", "rep", None, "tp"),
            P("fsdp", "tp"),
        ),
        check_vma=False,
    )
```

time: 463 us -> 260 us (0.56)
  waiting for transfers between devices: 350 us -> 185 us
  other arithmetic: 54.9 us -> 14.2 us
  starting transfers between devices: 0.16 us -> 15.3 us
  local copies, waits for them, and re-layouts: 11.7 us -> 26.6 us
  between operations: 13.9 us -> 0.91 us
  blocking collectives: 9.34 us -> 0 us
    ppermute x0 -> x13, waiting for transfers between devices: none -> 185 us  [swap(): return lax.ppermute(x, axis, SWAP)]
    psum x2 -> x0, waiting for transfers between devices: 181 us -> none  [the longest x1 147 us: per_device(): attn_total, norm_total = lax.psum((attn_terms, norm_terms), 'rep')]
    all_gather x2 -> x0, waiting for transfers between devices: 169 us -> none  [the longest x1 86.9 us: per_device(): lax.all_gather(new_emb_global, 'rep', axis=1, tiled=True)]
    reduce_or x1 -> x0, other arithmetic: 42 us -> none  [per_device(): touched_masks = jnp.any(matches, axis=1).astype(jnp.float32)]
    ppermute x0 -> x13, starting transfers between devices: none -> 15.3 us  [swap(): return lax.ppermute(x, axis, SWAP)]
    dynamic_update_slice x1 -> x7, local copies, waits for them, and re-layouts: 0.83 us -> 12.1 us  [the longest x4 8.97 us: per_device(): lax.dynamic_update_slice_in_dim(emb_weights, got, other_start + a, 0)]
    convert_element_type x3 -> x0, other arithmetic: 5.48 us -> none  [the longest x1 5.45 us: per_device(): attn_terms = attn_inner[0].astype(jnp.float32)]
    psum x1 -> x0, blocking collectives: 5.01 us -> none  [per_device(): attn_total, norm_total = lax.psum((attn_terms, norm_terms), 'rep')]
  transfers between devices with their start and end apart: 4 -> 13, of which waited for: 4 -> 7; matrix products, arithmetic and copies ran while one was open for 5% -> 13% of each run, Pallas kernels for 0% -> 0%
where the time goes in v1:
time: 260 us
  waiting for transfers between devices  185 us (71%)
  local copies, waits for them, and re-layouts  26.6 us (10%)
  matrix products  18.4 us (7%)
  starting transfers between devices  15.3 us (6%)
  other arithmetic  14.2 us (5%)
    ppermute x13, waiting for transfers between devices, swap(): return lax.ppermute(x, axis, SWAP)  185 us
    ppermute x13, starting transfers between devices, swap(): return lax.ppermute(x, axis, SWAP)  15.3 us
    unnamed x39, local copies, waits for them, and re-layouts  10.7 us
    dot_general x2, matrix products, coeff_of(): lax.dot_general(basis_half, rows, (((0,), (1,)), ((), ())), precision=lax...  9.63 us
    dynamic_update_slice x4, local copies, waits for them, and re-layouts, per_device(): lax.dynamic_update_slice_in_dim(emb_weights, got, other_start + a, 0)  8.97 us
    dot_general x1, matrix products, per_device(): lax.dot_general(coeff_sum, basis_half, (((0,), (1,)), ((), ())), precisio...  6.06 us
  transfers between devices with their start and end apart: 13, of which 7 were waited for; matrix products, arithmetic and copies ran while one was open for 13% of the time, Pallas kernels for 0%

profile of v1, /device:TPU:0, one launch (start us, length us, event | category | flops | bytes accessed | tf_op | source)
XLA Modules:
  0.0 260.0 jit_solution(9269443188040460845)
XLA Ops:
  0.6 0.0 copy-start
  0.7 1.1 multiply_subtract_fusion.2
  1.7 2.7 %fusion.18 = pred[1,2,16,256]{3,2,1,0:T(8,128)(4,1)S(1)} fusion(s32[2,8192]{1,0:T(2,128)S(1)} %get-tuple-element.11, s32[2,8192]{1,0:T(2,128)S(1)} %get-tuple-element.12), kind=kOutput, calls=%fused_computation.30 | convolution fusion | flops 138682368 | bytes 139264 | tf_op jit(solution)/shard_map/rht,rlt->rhl/dot_general | solution.py:37
  4.6 0.1 dynamic_slice.46
  4.6 0.0 copy-done
  4.6 5.9 %convolution_multiply_fusion = f32[64,4016]{1,0:T(8,128)S(1)} fusion(bf16[1,4016,512]{2,1,0:T(8,128)(2,1)} %param.19, f32[4016]{0:T(1024)S(1)} %bitcast.75, f32[1024,64]{0,1:T(8,128)S(1)} %copy-done, s32[]{:T(128)S(6)} %select_n.80), kind=kOutput, calls=%fused_computation.3 | convolution fusion | flops 1579412480 | bytes 5287940 | tf_op jit(solution)/shard_map/dot_general | solution.py:43
  10.5 0.2 negate_bitcast_fusion
  10.8 3.8 %fusion.12 = f32[1,64,2008]{2,1,0:T(8,128)S(1)} fusion(f32[1,1,2008,512]{3,2,1,0:T(8,128)S(1)} %copy-done.2, f32[64,4016]{1,0:T(8,128)S(1)} %convolution_multiply_fusion, s32[]{:T(128)S(6)} %select_n.79, f32[2008]{0:T(1024)S(1)} %dynamic_slice.46, f32[1024,64]{0,1:T(8,128)S(1)} %copy-done, s32[]{:T(128)S(6)} %select_n.80), kind=kOutput, calls=%fused_computation.14 | convolution fusion | flops 789834752 | bytes 5289992 | tf_op jit(solution)/shard_map/dot_general | solution.py:43
  14.6 0.5 collective-permute-start.6
  15.1 1.5 collective-permute-done.6
  16.6 0.1 fusion.21
  16.7 0.0 copy-start.18
  16.7 3.0 %collective-permute-start.7 = (f32[32,2008]{1,0:T(8,128)S(1)}, f32[32,2008]{1,0:T(8,128)S(1)}, u32[]{:S(2)}, u32[]{:S(2)}) collective-permute-start(f32[32,2008]{1,0:T(8,128)S(1)} %slice_bitcast_fusion), channel_id=1, source_target_pairs={{0,16},{16,0},{1,17},{17,1},{2,18},{18,2},{3,19},{19,3},{4,20},{20... | collective-permute-start | bytes 771080 | tf_op jit(solution)/shard_map/ppermute | solution.py:27
  19.7 3.5 %multiply_bitcast_fusion.1 = (f32[6,128,512]{2,1,0:T(8,128)}, f32[6,128,512]{2,1,0:T(8,128)}) fusion(bf16[1,24,128,512]{3,2,1,0:T(8,128)(2,1)} %param.13, s32[]{:T(128)S(6)} %select_n.72, s32[]{:T(128)S(6)} %select_n.74), kind=kLoop, calls=%fused_computation.24 | loop fusion | flops 1572864 | bytes 4718600 | tf_op jit(solution)/shard_map/div | solution.py:80
  23.1 0.0 collective-permute-start
  23.2 2.0 collective-permute-start.1
  25.2 1.5 collective-permute-done.7
  26.7 0.1 collective-permute-start.8
  26.8 2.2 collective-permute-start.4
  29.0 0.0 collective-permute-done.8
  29.1 0.0 copy-start.3
  29.1 0.0 copy-start.9
  29.1 1.0 broadcast_in_dim.8
  30.1 1.1 copy-done.3
  31.2 1.3 copy-done.9
  32.5 6.1 %constant_dynamic-update-slice_fusion.4 = (f32[4016,512]{1,0:T(8,128)S(1)}, f32[2008,512]{1,0:T(8,128)S(1)}, f32[1,1,2008,512]{3,2,1,0:T(8,128)}) fusion(f32[4016,512]{1,0:T(8,128)S(1)} %broadcast_in_dim.8, s32[]{:T(128)S(6)} %select_n.79, f32[1,1,2008,512]{3,2,1,0:T(8,128)S(1)} %copy-done.9, f32[1,1,2008,512]{3,2,1,0:T(8,128)S(1)} %copy-done.3, ...), kind=kOutput, calls=%fused_computation.60 | convolution fusion | flops 796902912 | bytes 21217288 | tf_op jit(solution)/shard_map/dot_general | solution.py:113
  38.6 3.3 %copy-done.5 = f32[4016,512]{1,0:T(8,128)} copy-done((f32[4016,512]{1,0:T(8,128)}, f32[4016,512]{1,0:T(8,128)S(1)}, u32[]{:S(2)}) %copy-start.5) | copy-done | bytes 8224792
  41.9 0.1 slice.53
  42.0 1.5 collective-permute-start.9
  43.5 17.2 %collective-permute-done = f32[6,128,512]{2,1,0:T(8,128)S(1)} collective-permute-done((f32[6,128,512]{2,1,0:T(8,128)}, f32[6,128,512]{2,1,0:T(8,128)S(1)}, u32[]{:S(2)}, u32[]{:S(2)}) %collective-permute-start) | collective-permute-done | bytes 1572896 | tf_op jit(solution)/shard_map/ppermute | solution.py:27
  60.6 1.1 copy-done.13
  61.8 32.7 %collective-permute-done.1 = f32[6,128,512]{2,1,0:T(8,128)} collective-permute-done((f32[6,128,512]{2,1,0:T(8,128)}, f32[6,128,512]{2,1,0:T(8,128)}, u32[]{:S(2)}, u32[]{:S(2)}) %collective-permute-start.1) | collective-permute-done | bytes 1572896 | tf_op jit(solution)/shard_map/ppermute | solution.py:27
  94.4 0.0 copy-done.12
  94.4 4.9 %multiply_subtract_fusion.1 = (f32[6,128,512]{2,1,0:T(8,128)S(1)}, f32[6,128,512]{2,1,0:T(8,128)}, f32[6,128,512]{2,1,0:T(8,128)S(1)}, f32[6,128,512]{2,1,0:T(8,128)}) fusion(f32[12,128,512]{2,1,0:T(8,128)S(1)} %copy-done.11, f32[6,128,512]{2,1,0:T(8,128)} %copy-done.13, bf16[1,24,128,512]{3,2,1,0:T(8,128)(2,1)S(1)} %copy-done.10, s32[]{:T(128)S(6)} %select_n.71, ...), kind=kLoop, calls=%fused_computation.22 | loop fusion | flops 7864320 | bytes 17301512 | tf_op jit(solution)/shard_map/sub | solution.py:16
  99.3 1.9 collective-permute-start.2
  101.2 0.0 copy-done.4
  101.2 1.8 fusion.37
  103.0 0.1 collective-permute-start.10
  103.1 1.9 collective-permute-start.3
  105.1 0.0 collective-permute-done.4
  105.1 0.6 constant_dynamic-update-slice_fusion.6
  105.7 0.1 collective-permute-start.5
  105.8 99.4 %collective-permute-done.5 = f32[2,512]{1,0:T(2,128)S(1)} collective-permute-done((f32[2,512]{1,0:T(2,128)S(1)}, f32[2,512]{1,0:T(2,128)S(1)}, u32[]{:S(2)}, u32[]{:S(2)}) %collective-permute-start.5) | collective-permute-done | bytes 4128 | tf_op jit(solution)/shard_map/ppermute | solution.py:27
  205.2 1.7 collective-permute-start.11
  207.0 0.0 collective-permute-done.9
  207.0 0.3 collective-permute-start.12
  207.3 0.8 broadcast_in_dim.6
  208.1 0.6 copy-done.6
  208.7 0.5 copy-done.7
  209.2 3.7 %constant_dynamic-update-slice_fusion.9 = (f32[24,128,512]{2,1,0:T(8,128)S(1)}, f32[12,128,512]{2,1,0:T(8,128)}, f32[12,128,512]{2,1,0:T(8,128)}) fusion(f32[24,128,512]{2,1,0:T(8,128)S(1)} %broadcast_in_dim.6, s32[]{:T(128)S(6)} %select_n.71, f32[6,128,512]{2,1,0:T(8,128)S(1)} %get-tuple-element.22, f32[6,128,512]{2,1,0:T(8,128)S(1)} %get-tuple-element.18, ...), kind=kLoop, calls=%fused_computation.70 | loop fusion | flops 1572864 | bytes 15728644 | tf_op jit(solution)/shard_map/dynamic_update_slice | solution.py:137
  212.9 2.2 constant_dynamic-update-slice_fusion.3
  215.1 0.0 collective-permute-done.10
  215.1 2.2 constant_dynamic-update-slice_fusion.2
  217.4 13.9 %collective-permute-done.11 = f32[504,512]{1,0:T(8,128)} collective-permute-done((f32[504,512]{1,0:T(8,128)}, f32[504,512]{1,0:T(8,128)}, u32[]{:S(2)}, u32[]{:S(2)}) %collective-permute-start.11) | collective-permute-done | bytes 1032224 | tf_op jit(solution)/shard_map/ppermute | solution.py:27
  231.3 2.2 constant_dynamic-update-slice_fusion.1
  233.5 18.4 %collective-permute-done.12 = f32[504,512]{1,0:T(8,128)} collective-permute-done((f32[504,512]{1,0:T(8,128)}, f32[504,512]{1,0:T(8,128)}, u32[]{:S(2)}, u32[]{:S(2)}) %collective-permute-start.12) | collective-permute-done | bytes 1032224 | tf_op jit(solution)/shard_map/ppermute | solution.py:27
  251.9 2.2 constant_dynamic-update-slice_fusion
  254.1 0.0 collective-permute-done.2
  254.2 1.6 constant_dynamic-update-slice_fusion.8
  255.7 0.0 collective-permute-done.3
  255.7 1.5 constant_dynamic-update-slice_fusion.7
  257.3 0.0 copy-start.8
  257.3 2.7 %copy-done.8 = f32[24,128,512]{2,1,0:T(8,128)} copy-done((f32[24,128,512]{2,1,0:T(8,128)}, f32[24,128,512]{2,1,0:T(8,128)S(1)}, u32[]{:S(2)}) %copy-start.8) | copy-done | bytes 6291480
  260.0 0.0 copy-done.1
  (33 shorter events, 0.3 us)
Async XLA Ops:
  0.6 4.0 %copy-start = (f32[1024,64]{0,1:T(8,128)S(1)}, f32[1024,64]{0,1:T(8,128)}, u32[]{:S(2)}) copy-start(f32[1024,64]{0,1:T(8,128)} %param.20) | copy-start | bytes 786436
  4.6 6.1 %copy-start.2 = (f32[1,1,2008,512]{3,2,1,0:T(8,128)S(1)}, f32[1,1,2008,512]{3,2,1,0:T(8,128)}, u32[]{:S(2)}) copy-start(f32[1,1,2008,512]{3,2,1,0:T(8,128)} %param.17) | copy-start | bytes 12337156
  14.6 2.1 collective-permute-start.6
  16.7 10.1 %copy-start.18 = (bf16[1,4,512]{2,1,0:T(4,128)(2,1)S(1)}, bf16[1,4,512]{2,1,0:T(4,128)(2,1)}, u32[]{:S(2)}) copy-start(bf16[1,4,512]{2,1,0:T(4,128)(2,1)} %param.16) | copy-start | bytes 12292
  16.7 10.0 %collective-permute-start.7 = (f32[32,2008]{1,0:T(8,128)S(1)}, f32[32,2008]{1,0:T(8,128)S(1)}, u32[]{:S(2)}, u32[]{:S(2)}) collective-permute-start(f32[32,2008]{1,0:T(8,128)S(1)} %slice_bitcast_fusion), channel_id=1, source_target_pairs={{0,16},{16,0},{1,17},{17,1},{2,18},{18,2},{3,19},{19,3},{4,20},{20... | collective-permute-start | bytes 771080 | tf_op jit(solution)/shard_map/ppermute | solution.py:27
  23.1 37.5 %collective-permute-start = (f32[6,128,512]{2,1,0:T(8,128)}, f32[6,128,512]{2,1,0:T(8,128)S(1)}, u32[]{:S(2)}, u32[]{:S(2)}) collective-permute-start(f32[6,128,512]{2,1,0:T(8,128)} %get-tuple-element.28), channel_id=1, source_target_pairs={{0,16},{16,0},{1,17},{17,1},{2,18},{18,2},{3,19},{19,3},{4,20},{20... | collective-permute-start | bytes 4718600 | tf_op jit(solution)/shard_map/ppermute | solution.py:27
  23.2 71.3 %collective-permute-start.1 = (f32[6,128,512]{2,1,0:T(8,128)}, f32[6,128,512]{2,1,0:T(8,128)}, u32[]{:S(2)}, u32[]{:S(2)}) collective-permute-start(f32[6,128,512]{2,1,0:T(8,128)} %get-tuple-element.29), channel_id=1, source_target_pairs={{0,16},{16,0},{1,17},{17,1},{2,18},{18,2},{3,19},{19,3},{4,20},{20... | collective-permute-start | bytes 4718600 | tf_op jit(solution)/shard_map/ppermute | solution.py:27
  26.7 2.3 collective-permute-start.8
  26.8 78.2 %collective-permute-start.4 = (f32[2,512]{1,0:T(2,128)S(1)}, f32[2,512]{1,0:T(2,128)S(1)}, u32[]{:S(2)}, u32[]{:S(2)}) collective-permute-start(f32[2,512]{1,0:T(2,128)S(1)} %multiply_bitcast_fusion.2), channel_id=1, source_target_pairs={{0,16},{16,0},{1,17},{17,1},{2,18},{18,2},{3,19},{19,3},{4,20},{20... | collective-permute-start | bytes 12296 | tf_op jit(solution)/shard_map/ppermute | solution.py:27
  29.1 2.2 copy-start.3
  29.1 3.4 %copy-start.9 = (f32[1,1,2008,512]{3,2,1,0:T(8,128)S(1)}, f32[1,1,2008,512]{3,2,1,0:T(8,128)}, u32[]{:S(2)}) copy-start(f32[1,1,2008,512]{3,2,1,0:T(8,128)} %param.18) | copy-start | bytes 12337156
  32.5 61.9 %copy-start.10 = (bf16[1,24,128,512]{3,2,1,0:T(8,128)(2,1)S(1)}, bf16[1,24,128,512]{3,2,1,0:T(8,128)(2,1)}, u32[]{:S(2)}) copy-start(bf16[1,24,128,512]{3,2,1,0:T(8,128)(2,1)} %param.13) | copy-start | bytes 9437188
  32.5 61.9 %copy-start.11 = (f32[12,128,512]{2,1,0:T(8,128)S(1)}, f32[12,128,512]{2,1,0:T(8,128)}, u32[]{:S(2)}) copy-start(f32[12,128,512]{2,1,0:T(8,128)} %param.11) | copy-start | bytes 9437188
  32.5 61.9 %copy-start.12 = (f32[12,128,512]{2,1,0:T(8,128)S(1)}, f32[12,128,512]{2,1,0:T(8,128)}, u32[]{:S(2)}) copy-start(f32[12,128,512]{2,1,0:T(8,128)} %param.12) | copy-start | bytes 9437188
  38.6 3.3 %copy-start.5 = (f32[4016,512]{1,0:T(8,128)}, f32[4016,512]{1,0:T(8,128)S(1)}, u32[]{:S(2)}) copy-start(f32[4016,512]{1,0:T(8,128)S(1)} %get-tuple-element.9) | copy-start | bytes 24674308
  41.9 59.3 %copy-start.4 = (f32[2008,512]{1,0:T(8,128)}, f32[2008,512]{1,0:T(8,128)S(1)}, u32[]{:S(2)}) copy-start(f32[2008,512]{1,0:T(8,128)S(1)} %get-tuple-element.10) | copy-start | bytes 12337156
  42.0 165.0 %collective-permute-start.9 = (f32[496,512]{1,0:T(8,128)S(1)}, f32[496,512]{1,0:T(8,128)}, u32[]{:S(2)}, u32[]{:S(2)}) collective-permute-start(f32[496,512]{1,0:T(8,128)S(1)} %slice.53), channel_id=1, source_target_pairs={{0,16},{16,0},{1,17},{17,1},{2,18},{18,2},{3,19},{19,3},{4,20},{20... | collective-permute-start | bytes 3047432 | tf_op jit(solution)/shard_map/ppermute | solution.py:27
  60.6 1.1 copy-start.13
  99.3 5.7 %copy-start.15 = (f32[2,512]{1,0:T(2,128)S(1)}, f32[2,512]{1,0:T(2,128)}, u32[]{:S(2)}) copy-start(f32[2,512]{1,0:T(2,128)} %param.14) | copy-start | bytes 12292
  99.3 5.7 %copy-start.16 = (f32[2,512]{1,0:T(2,128)S(1)}, f32[2,512]{1,0:T(2,128)}, u32[]{:S(2)}) copy-start(f32[2,512]{1,0:T(2,128)} %param.15) | copy-start | bytes 12292
  99.3 154.8 %collective-permute-start.2 = (f32[6,128,512]{2,1,0:T(8,128)S(1)}, f32[6,128,512]{2,1,0:T(8,128)}, u32[]{:S(2)}, u32[]{:S(2)}) collective-permute-start(f32[6,128,512]{2,1,0:T(8,128)S(1)} %get-tuple-element.18), channel_id=1, source_target_pairs={{0,16},{16,0},{1,17},{17,1},{2,18},{18,2},{3,19},{19,3},{4,20},{20... | collective-permute-start | bytes 4718600 | tf_op jit(solution)/shard_map/ppermute | solution.py:27
  103.0 112.1 %collective-permute-start.10 = (f32[504,512]{1,0:T(8,128)}, f32[504,512]{1,0:T(8,128)}, u32[]{:S(2)}, u32[]{:S(2)}) collective-permute-start(f32[504,512]{1,0:T(8,128)} %get-tuple-element.27), channel_id=1, source_target_pairs={{0,16},{16,0},{1,17},{17,1},{2,18},{18,2},{3,19},{19,3},{4,20},{20... | collective-permute-start | bytes 3096584 | tf_op jit(solution)/shard_map/ppermute | solution.py:27
  103.1 152.6 %collective-permute-start.3 = (f32[6,128,512]{2,1,0:T(8,128)S(1)}, f32[6,128,512]{2,1,0:T(8,128)}, u32[]{:S(2)}, u32[]{:S(2)}) collective-permute-start(f32[6,128,512]{2,1,0:T(8,128)S(1)} %get-tuple-element.22), channel_id=1, source_target_pairs={{0,16},{16,0},{1,17},{17,1},{2,18},{18,2},{3,19},{19,3},{4,20},{20... | collective-permute-start | bytes 4718600 | tf_op jit(solution)/shard_map/ppermute | solution.py:27
  105.7 102.4 %copy-start.17 = (f32[2,512]{1,0:T(2,128)}, f32[2,512]{1,0:T(2,128)S(1)}, u32[]{:S(2)}) copy-start(f32[2,512]{1,0:T(2,128)S(1)} %get-tuple-element.14) | copy-start | bytes 12292
  105.7 99.5 %collective-permute-start.5 = (f32[2,512]{1,0:T(2,128)S(1)}, f32[2,512]{1,0:T(2,128)S(1)}, u32[]{:S(2)}, u32[]{:S(2)}) collective-permute-start(f32[2,512]{1,0:T(2,128)S(1)} %get-tuple-element.14), channel_id=1, source_target_pairs={{0,16},{16,0},{1,17},{17,1},{2,18},{18,2},{3,19},{19,3},{4,20},{20... | collective-permute-start | bytes 12296 | tf_op jit(solution)/shard_map/ppermute | solution.py:27
  205.2 26.1 %collective-permute-start.11 = (f32[504,512]{1,0:T(8,128)}, f32[504,512]{1,0:T(8,128)}, u32[]{:S(2)}, u32[]{:S(2)}) collective-permute-start(f32[504,512]{1,0:T(8,128)} %get-tuple-element.26), channel_id=1, source_target_pairs={{0,16},{16,0},{1,17},{17,1},{2,18},{18,2},{3,19},{19,3},{4,20},{20... | collective-permute-start | bytes 3096584 | tf_op jit(solution)/shard_map/ppermute | solution.py:27
  207.0 44.9 %collective-permute-start.12 = (f32[504,512]{1,0:T(8,128)}, f32[504,512]{1,0:T(8,128)}, u32[]{:S(2)}, u32[]{:S(2)}) collective-permute-start(f32[504,512]{1,0:T(8,128)} %get-tuple-element.25), channel_id=1, source_target_pairs={{0,16},{16,0},{1,17},{17,1},{2,18},{18,2},{3,19},{19,3},{4,20},{20... | collective-permute-start | bytes 3096584 | tf_op jit(solution)/shard_map/ppermute | solution.py:27
  207.3 0.8 copy-start.14
  207.3 1.4 copy-start.6
  207.3 1.9 copy-start.7
  254.1 5.8 %copy-start.1 = (f32[1024,64]{0,1:T(8,128)S(1)}, f32[1024,64]{0,1:T(8,128)}, u32[]{:S(2)}) copy-start(f32[1024,64]{0,1:T(8,128)} %param.20) | copy-start | bytes 786436
  257.3 2.7 %copy-start.8 = (f32[24,128,512]{2,1,0:T(8,128)}, f32[24,128,512]{2,1,0:T(8,128)S(1)}, u32[]{:S(2)}) copy-start(f32[24,128,512]{2,1,0:T(8,128)S(1)} %constant_dynamic-update-slice_fusion.7) | copy-start | bytes 18874372

commit v2 on v1

v2 whole, which is shorter than its diff:
```python
import jax
import jax.numpy as jnp
from jax import lax
from jax.sharding import PartitionSpec as P

OUTER_RATE = 0.7
MOMENTUM = 0.9
SWAP = ((0, 1), (1, 0))
EMB_CUTS = (0, 3, 6, 9, 12)
TWELFTHS = 12
LOW = 256


def nesterov(global_part, momentum_part, outer_grad):
    fresh_momentum = MOMENTUM * momentum_part + outer_grad
    fresh_global = global_part - OUTER_RATE * (outer_grad + MOMENTUM * fresh_momentum)
    return (fresh_global, fresh_momentum)


def cuts(total, marks, unit):
    units = -(-total // unit)
    bounds = [min(total, unit * (units * mark // TWELFTHS)) for mark in marks]
    return [(a, b) for a, b in zip(bounds[:-1], bounds[1:]) if b > a]


def swap(x, axis):
    return lax.ppermute(x, axis, SWAP)


def after(x, earlier):
    return lax.optimization_barrier((x, earlier))[0]


def placed(own, rep_index):
    halves = jnp.zeros((2,) + own.shape, jnp.float32)
    return lax.dynamic_update_slice(halves, own[None], (rep_index,) + (0,) * own.ndim)


def put(halves, piece, at, rep_index):
    return lax.dynamic_update_slice(halves, piece[None], (1 - rep_index, at) + (0,) * (piece.ndim - 1))


def row_masks(touched, row_start, block_rows):
    high_count = -(-block_rows // LOW)
    local = touched - row_start
    high = jnp.floor_divide(local, LOW)
    low = local - high * LOW
    high_hot = (high[:, None, :] == jnp.arange(high_count, dtype=jnp.int32)[None, :, None]).astype(jnp.bfloat16)
    low_hot = (low[:, None, :] == jnp.arange(LOW, dtype=jnp.int32)[None, :, None]).astype(jnp.bfloat16)
    times = jnp.einsum("rht,rlt->rhl", high_hot, low_hot, preferred_element_type=jnp.float32)
    masks = (times > 0.5).astype(jnp.float32)
    return masks.reshape(touched.shape[0], high_count * LOW)[:, :block_rows]


def coeff_of(rows, basis_half):
    return lax.dot_general(
        basis_half,
        rows,
        (((0,), (1,)), ((), ())),
        precision=lax.Precision.HIGHEST,
        preferred_element_type=jnp.float32,
    )


def per_device(
    attn_global,
    attn_momentum,
    attn_inner,
    norm_global,
    norm_momentum,
    norm_inner,
    emb_global,
    emb_momentum,
    emb_inner,
    basis,
    touched,
):
    groups = lax.axis_size("rep") * 1.0
    rep_index = lax.axis_index("rep")
    tp_index = lax.axis_index("tp")
    other = 1 - rep_index
    attn_owned = attn_global.shape[0]
    norm_owned = norm_global.shape[0]
    block_rows = emb_inner.shape[1]
    half_rows = emb_global.shape[2]
    half_width = emb_global.shape[3]
    rank = basis.shape[1]

    width = attn_global.shape[2]

    def pack(attn, norm):
        return jnp.concatenate((attn.reshape(-1, width), norm), axis=0)

    def unpack(rows):
        return rows[:-norm_owned].reshape(attn_global.shape), rows[-norm_owned:]

    def mean_part(inner, owned, owner):
        part = lax.dynamic_slice_in_dim(inner[0], owner * owned, owned, 0)
        return part.astype(jnp.float32) / groups

    leaving = pack(mean_part(attn_inner, attn_owned, other), mean_part(norm_inner, norm_owned, other))
    arrived = swap(leaving, "rep")

    touched = after(touched, leaving)
    masks = row_masks(touched, lax.axis_index("fsdp") * block_rows, block_rows)
    masks = masks.reshape(masks.shape[0], 2, half_rows)
    own_mask = lax.dynamic_index_in_dim(masks, rep_index, 0, keepdims=False)
    half_counts = lax.dynamic_index_in_dim(jnp.sum(masks, axis=0), rep_index, 0, keepdims=False)
    mask_kept = lax.dynamic_index_in_dim(own_mask, rep_index, 0, keepdims=False)
    mask_given = lax.dynamic_index_in_dim(own_mask, other, 0, keepdims=False)
    basis_half = lax.dynamic_slice_in_dim(basis, tp_index * half_width, half_width, 0)
    own_rows = emb_global[0, 0]
    own_momentum = emb_momentum[0, 0]
    inner_halves = emb_inner[0].reshape(2, half_rows, half_width)
    inner_kept = lax.dynamic_index_in_dim(inner_halves, rep_index, 0, keepdims=False)
    inner_given = lax.dynamic_index_in_dim(inner_halves, other, 0, keepdims=False)
    half_rank = rank // 2
    terms = jnp.stack(
        (
            half_counts[None, :] * coeff_of(own_rows, basis_half)
            - mask_kept[None, :] * coeff_of(inner_kept.astype(jnp.float32), basis_half),
            -mask_given[None, :] * coeff_of(inner_given.astype(jnp.float32), basis_half),
        )
    )
    kept = lax.dynamic_slice_in_dim(terms, tp_index * half_rank, half_rank, 1)
    given = lax.dynamic_slice_in_dim(terms, (1 - tp_index) * half_rank, half_rank, 1)
    summed = kept + swap(given, "tp")
    coeff_arrived = swap(summed[1], "rep")

    attn_arrived, norm_arrived = unpack(after(arrived, summed))
    attn_mean = mean_part(attn_inner, attn_owned, rep_index) + attn_arrived
    norm_mean = mean_part(norm_inner, norm_owned, rep_index) + norm_arrived
    new_attn_global, new_attn_momentum = nesterov(attn_global, attn_momentum, attn_global - attn_mean)
    new_norm_global, new_norm_momentum = nesterov(norm_global, norm_momentum, norm_global - norm_mean)
    back = pack(new_attn_global, new_norm_global)
    returned = swap(back, "rep")

    coeff_mine = summed[0] + after(coeff_arrived, back)
    coeff_theirs = swap(coeff_mine, "tp")
    first = tp_index == 0
    coeff_sum = jnp.concatenate(
        (
            jnp.where(first, coeff_mine, coeff_theirs),
            jnp.where(first, coeff_theirs, coeff_mine),
        ),
        axis=0,
    )
    emb_grad = (
        lax.dot_general(
            coeff_sum,
            basis_half,
            (((0,), (1,)), ((), ())),
            precision=lax.Precision.HIGHEST,
            preferred_element_type=jnp.float32,
        )
        / groups
    )
    fresh_rows, fresh_momentum = nesterov(own_rows, own_momentum, emb_grad)
    emb_cuts = cuts(half_rows, EMB_CUTS, 8)
    emb_returned = [swap(fresh_rows[a:b], "rep") for a, b in emb_cuts]

    attn_returned, norm_returned = unpack(returned)
    attn_weights = put(placed(new_attn_global, rep_index), attn_returned, 0, rep_index)
    norm_weights = put(placed(new_norm_global, rep_index), norm_returned, 0, rep_index)
    emb_weights = placed(fresh_rows, rep_index)
    for i, ((a, _), got) in enumerate(zip(emb_cuts, emb_returned)):
        if i >= 1:
            got = after(got, (attn_weights, norm_weights))
        emb_weights = put(emb_weights, got, a, rep_index)
    attn_weights, norm_weights, emb_weights = [
        halves.reshape((-1,) + halves.shape[2:]) for halves in (attn_weights, norm_weights, emb_weights)
    ]

    return (
        new_attn_global,
        new_attn_momentum,
        attn_weights,
        new_norm_global,
        new_norm_momentum,
        norm_weights,
        fresh_rows.reshape(emb_global.shape),
        fresh_momentum.reshape(emb_momentum.shape),
        emb_weights,
    )


def solution(mesh):
    placed = (
        P("rep", "fsdp", "tp"),
        P("rep", "fsdp", "tp"),
        P("rep", None, "fsdp", "tp"),
        P("rep", "tp"),
        P("rep", "tp"),
        P("rep", None, "tp"),
        P("fsdp", "rep", None, "tp"),
        P("fsdp", "rep", None, "tp"),
        P("rep", "fsdp", "tp"),
        P(),
        P(),
    )
    return jax.shard_map(
        per_device,
        mesh=mesh,
        in_specs=placed,
        out_specs=(
            P("rep", "fsdp", "tp"),
            P("rep", "fsdp", "tp"),
            P(None, "fsdp", "tp"),
            P("rep", "tp"),
            P("rep", "tp"),
            P(None, "tp"),
            P("fsdp", "rep", None, "tp"),
            P("fsdp", "rep", None, "tp"),
            P("fsdp", "tp"),
        ),
        check_vma=False,
    )
```

time: 260 us -> 253 us (0.973)
  starting transfers between devices: 15.3 us -> 8.34 us
  waiting for transfers between devices: 185 us -> 179 us
  other arithmetic: 14.2 us -> 19.9 us
    ppermute x13 -> x9, starting transfers between devices: 15.3 us -> 8.34 us  [swap(): return lax.ppermute(x, axis, SWAP)]
    unnamed x39 -> x31, local copies, waits for them, and re-layouts: 10.7 us -> 4.72 us
    ppermute x13 -> x9, waiting for transfers between devices: 185 us -> 179 us  [swap(): return lax.ppermute(x, axis, SWAP)]
    dynamic_update_slice x7 -> x6, local copies, waits for them, and re-layouts: 12.1 us -> 6.8 us  [put(): lax.dynamic_update_slice(halves, piece[None], (1 - rep_index, at) + (0,)...]
    sub x1 -> x0, other arithmetic: 4.89 us -> none  [nesterov(): global_part - OUTER_RATE * (outer_grad + MOMENTUM * fresh_momentum)]
    slice x2 -> x4, local copies, waits for them, and re-layouts: 1.84 us -> 6.43 us  [the longest x2 4.39 us: unpack(): return (rows[:-norm_owned].reshape(attn_global.shape), rows[-norm_owned:])]
    broadcast_in_dim x3, local copies, waits for them, and re-layouts: 1.83 us -> 6.02 us  [placed(): halves = jnp.zeros((2,) + own.shape, jnp.float32)]
    concatenate x0 -> x2, other arithmetic: none -> 4.12 us  [pack(): return jnp.concatenate((attn.reshape(-1, width), norm), axis=0)]
  transfers between devices with their start and end apart: 13 -> 9, of which waited for: 7 -> 7; matrix products, arithmetic and copies ran while one was open for 13% -> 21% of each run, Pallas kernels for 0% -> 0%
where the time goes in v2:
time: 253 us
  waiting for transfers between devices  179 us (71%)
  local copies, waits for them, and re-layouts  25.6 us (10%)
  other arithmetic  19.9 us (8%)
  matrix products  19.2 us (8%)
  starting transfers between devices  8.34 us (3%)
    ppermute x9, waiting for transfers between devices, swap(): return lax.ppermute(x, axis, SWAP)  179 us
    dot_general x3, matrix products, coeff_of(): lax.dot_general(basis_half, rows, (((0,), (1,)), ((), ())), precision=lax...  10.7 us
    ppermute x9, starting transfers between devices, swap(): return lax.ppermute(x, axis, SWAP)  8.34 us
    dynamic_update_slice x2, other arithmetic, placed(): lax.dynamic_update_slice(halves, own[None], (rep_index,) + (0,) * own.ndim)  7.06 us
    dynamic_update_slice x6, local copies, waits for them, and re-layouts, put(): lax.dynamic_update_slice(halves, piece[None], (1 - rep_index, at) + (0,)...  6.8 us
    broadcast_in_dim x3, local copies, waits for them, and re-layouts, placed(): halves = jnp.zeros((2,) + own.shape, jnp.float32)  6.02 us
    dot_general x1, matrix products, per_device(): lax.dot_general(coeff_sum, basis_half, (((0,), (1,)), ((), ())), precisio...  5.83 us
  transfers between devices with their start and end apart: 9, of which 7 were waited for; matrix products, arithmetic and copies ran while one was open for 21% of the time, Pallas kernels for 0%

profile of v2, /device:TPU:0, one launch (start us, length us, event | category | flops | bytes accessed | tf_op | source)
XLA Modules:
  0.0 253.0 jit_solution(2847911026274763894)
XLA Ops:
  0.6 0.0 copy-start
  0.7 0.7 multiply_bitcast_fusion
  1.4 1.8 convert_multiply_fusion
  3.2 0.0 copy-start.10
  3.2 2.0 pad_maximum_fusion
  5.2 3.0 %collective-permute-start = (f32[1538,512]{1,0:T(8,128)}, f32[1538,512]{1,0:T(8,128)}, u32[]{:S(2)}, u32[]{:S(2)}) collective-permute-start(f32[1538,512]{1,0:T(8,128)} %pad_maximum_fusion), channel_id=1, source_target_pairs={{0,16},{16,0},{1,17},{17,1},{2,18},{18,2},{3,19},{19,3},{4,20},{20... | collective-permute-start | bytes 9449480 | tf_op jit(solution)/shard_map/ppermute | solution.py:27
  8.2 0.2 multiply_subtract_fusion.1
  8.4 2.7 %fusion.21 = pred[1,2,16,256]{3,2,1,0:T(8,128)(4,1)S(1)} fusion(s32[2,8192]{1,0:T(2,128)S(1)} %get-tuple-element.29, s32[2,8192]{1,0:T(2,128)S(1)} %get-tuple-element.30), kind=kOutput, calls=%fused_computation.32 | convolution fusion | flops 138682368 | bytes 139264 | tf_op jit(solution)/shard_map/rht,rlt->rhl/dot_general | solution.py:50
  11.2 0.1 reduce_sum.12
  11.3 0.1 reshape.81
  11.4 0.0 copy-start.3
  11.4 3.6 %fusion.15 = f32[1,64,2008]{2,1,0:T(8,128)S(1)} fusion(bf16[2,2008,512]{2,1,0:T(8,128)(2,1)} %bitcast.96, s32[]{:T(128)S(6)} %select_n.71, f32[2008]{0:T(1024)S(1)} %bitcast.102, f32[1024,64]{0,1:T(8,128)S(1)} %copy-done, s32[]{:T(128)S(6)} %select_n.69), kind=kOutput, calls=%fused_computation.22 | convolution fusion | flops 789706240 | bytes 2709512 | tf_op jit(solution)/shard_map/dot_general | solution.py:56
  15.0 3.4 %convolution_multiply_fusion.1 = f32[64,2008]{1,0:T(8,128)S(1)} fusion(bf16[2,2008,512]{2,1,0:T(8,128)(2,1)} %bitcast.97, s32[]{:T(128)S(6)} %select_n.68, f32[2008]{0:T(1024)S(1)} %bitcast.101, f32[1024,64]{0,1:T(8,128)S(1)} %copy-done, s32[]{:T(128)S(6)} %select_n.69), kind=kOutput, calls=%fused_computation.21 | convolution fusion | flops 789706240 | bytes 2709512 | tf_op jit(solution)/shard_map/dot_general | solution.py:56
  18.5 3.8 %fusion.12 = f32[1,64,2008]{2,1,0:T(8,128)S(1)} fusion(f32[64,2008]{1,0:T(8,128)S(1)} %convolution_multiply_fusion.1, f32[1,1,2008,512]{3,2,1,0:T(8,128)S(1)} %copy-done.3, f32[2008]{0:T(1024)S(1)} %bitcast.100, f32[1024,64]{0,1:T(8,128)S(1)} %copy-done, s32[]{:T(128)S(6)} %select_n.69), kind=kOutput, calls=%fused_computation.19 | convolution fusion | flops 789834752 | bytes 5289988 | tf_op jit(solution)/shard_map/dot_general | solution.py:56
  22.3 0.1 collective-permute-start.1
  22.4 0.0 copy-start.12
  22.4 0.0 copy-start.13
  22.4 0.0 copy-start.14
  22.4 1.9 collective-permute-done.1
  24.3 0.1 fusion.24
  24.3 0.0 copy-start.8
  24.3 0.8 slice_bitcast_fusion
  25.1 0.0 collective-permute-start.3
  25.1 0.1 copy-done.8
  25.2 52.6 %collective-permute-done = f32[1538,512]{1,0:T(8,128)} collective-permute-done((f32[1538,512]{1,0:T(8,128)}, f32[1538,512]{1,0:T(8,128)}, u32[]{:S(2)}, u32[]{:S(2)}) %collective-permute-start) | collective-permute-done | bytes 3149856 | tf_op jit(solution)/shard_map/ppermute | solution.py:27
  77.8 2.2 slice.38
  80.0 0.0 copy-start.7
  80.0 1.5 constant_dynamic-update-slice_fusion.1
  81.5 0.8 broadcast_in_dim.40
  82.3 5.6 %bitcast_dynamic-update-slice_fusion.1 = (f32[2,12,128,512]{3,2,1,0:T(8,128)S(1)}, f32[12,128,512]{2,1,0:T(8,128)S(1)}, f32[12,128,512]{2,1,0:T(8,128)}) fusion(f32[2,12,128,512]{3,2,1,0:T(8,128)S(1)} %broadcast_in_dim.40, s32[]{:T(128)S(6)} %select_n.68, f32[12,128,512]{2,1,0:T(8,128)S(1)} %copy-done.7, f32[12,128,512]{2,1,0:T(8,128)S(1)} %bitcast.91, ...), kind=kLoop, calls=%fused_computation.11 | loop fusion | flops 7864320 | bytes 20447240 | tf_op jit(solution)/shard_map/dynamic_update_slice | solution.py:36
  87.9 2.7 %copy-done.6 = f32[2,12,128,512]{3,2,1,0:T(8,128)} copy-done((f32[2,12,128,512]{3,2,1,0:T(8,128)}, f32[2,12,128,512]{3,2,1,0:T(8,128)S(1)}, u32[]{:S(2)}) %copy-start.6) | copy-done | bytes 6291480
  90.6 2.1 pad_maximum_fusion.1
  92.8 2.1 collective-permute-start.2
  94.8 0.0 collective-permute-done.3
  94.8 1.7 fusion.30
  96.5 0.0 collective-permute-start.4
  96.5 1.9 collective-permute-done.4
  98.4 1.1 broadcast_select_fusion.1
  99.5 0.0 copy-start.1
  99.5 0.0 copy-start.4
  99.5 5.2 %broadcast_in_dim.45 = f32[2,2008,512]{2,1,0:T(8,128)} broadcast(f32[]{:T(128)} %constant.124.clone.1), dimensions={} | broadcast | bytes 8224772 | tf_op jit(solution)/shard_map/broadcast_in_dim | solution.py:35
  104.7 1.1 copy-done.4
  105.9 5.8 %bitcast_dynamic-update-slice_fusion = (f32[2,2008,512]{2,1,0:T(8,128)}, f32[2008,512]{1,0:T(8,128)S(1)}, f32[2008,512]{1,0:T(8,128)S(1)}) fusion(f32[2,2008,512]{2,1,0:T(8,128)} %broadcast_in_dim.45, s32[]{:T(128)S(6)} %select_n.68, f32[1,1,2008,512]{3,2,1,0:T(8,128)S(1)} %copy-done.1, f32[1,1,2008,512]{3,2,1,0:T(8,128)S(1)} %copy-done.4, ...), kind=kOutput, calls=%fused_computation.3 | convolution fusion | flops 796902912 | bytes 21217288 | tf_op jit(solution)/shard_map/dot_general | solution.py:149
  111.7 0.1 slice.53
  111.8 0.2 collective-permute-start.5
  112.0 2.0 fusion.42
  113.9 0.7 copy-done.2
  114.6 1.0 collective-permute-start.8
  115.6 1.0 collective-permute-start.7
  116.7 1.0 collective-permute-start.6
  117.7 3.0 %fusion.4 = f32[1,1,2008,512]{3,2,1,0:T(8,128)} fusion(f32[2008,512]{1,0:T(8,128)S(1)} %get-tuple-element.38, f32[1,1,2008,512]{3,2,1,0:T(8,128)S(1)} %copy-done.1), kind=kLoop, calls=%fused_computation.8 | loop fusion | flops 3084288 | bytes 12337152 | tf_op jit(solution)/shard_map/reshape | solution.py:182
  120.7 65.5 %collective-permute-done.5 = f32[496,512]{1,0:T(8,128)S(1)} collective-permute-done((f32[496,512]{1,0:T(8,128)S(1)}, f32[496,512]{1,0:T(8,128)S(1)}, u32[]{:S(2)}, u32[]{:S(2)}) %collective-permute-start.5) | collective-permute-done | bytes 1015840 | tf_op jit(solution)/shard_map/ppermute | solution.py:27
  186.2 1.0 bitcast_dynamic-update-slice_fusion.5
  187.2 0.0 collective-permute-done.2
  187.2 0.7 constant_dynamic-update-slice_fusion
  187.9 0.6 reshape.85
  188.5 2.2 slice.49
  190.7 2.0 constant_dynamic-update-slice_fusion.2
  192.7 15.6 %collective-permute-done.8 = f32[504,512]{1,0:T(8,128)S(1)} collective-permute-done((f32[504,512]{1,0:T(8,128)}, f32[504,512]{1,0:T(8,128)S(1)}, u32[]{:S(2)}, u32[]{:S(2)}) %collective-permute-start.8) | collective-permute-done | bytes 1032224 | tf_op jit(solution)/shard_map/ppermute | solution.py:27
  208.3 22.1 %collective-permute-done.7 = f32[504,512]{1,0:T(8,128)S(1)} collective-permute-done((f32[504,512]{1,0:T(8,128)}, f32[504,512]{1,0:T(8,128)S(1)}, u32[]{:S(2)}, u32[]{:S(2)}) %collective-permute-start.7) | collective-permute-done | bytes 1032224 | tf_op jit(solution)/shard_map/ppermute | solution.py:27
  230.4 19.5 %collective-permute-done.6 = f32[504,512]{1,0:T(8,128)S(1)} collective-permute-done((f32[504,512]{1,0:T(8,128)}, f32[504,512]{1,0:T(8,128)S(1)}, u32[]{:S(2)}, u32[]{:S(2)}) %collective-permute-start.6) | collective-permute-done | bytes 1032224 | tf_op jit(solution)/shard_map/ppermute | solution.py:27
  249.9 1.0 bitcast_dynamic-update-slice_fusion.4
  250.9 1.0 bitcast_dynamic-update-slice_fusion.3
  252.0 1.0 bitcast_dynamic-update-slice_fusion.2
  (23 shorter events, 0.2 us)
Async XLA Ops:
  0.6 10.8 %copy-start = (f32[1024,64]{0,1:T(8,128)S(1)}, f32[1024,64]{0,1:T(8,128)}, u32[]{:S(2)}) copy-start(f32[1024,64]{0,1:T(8,128)} %param.20) | copy-start | bytes 786436
  3.2 5.0 %copy-start.10 = (s32[2,8192]{1,0:T(2,128)S(1)}, s32[2,8192]{1,0:T(2,128)}, u32[]{:S(2)}) copy-start(s32[2,8192]{1,0:T(2,128)} %param.21) | copy-start | bytes 196612
  5.2 72.6 %collective-permute-start = (f32[1538,512]{1,0:T(8,128)}, f32[1538,512]{1,0:T(8,128)}, u32[]{:S(2)}, u32[]{:S(2)}) collective-permute-start(f32[1538,512]{1,0:T(8,128)} %pad_maximum_fusion), channel_id=1, source_target_pairs={{0,16},{16,0},{1,17},{17,1},{2,18},{18,2},{3,19},{19,3},{4,20},{20... | collective-permute-start | bytes 9449480 | tf_op jit(solution)/shard_map/ppermute | solution.py:27
  11.4 7.1 %copy-start.3 = (f32[1,1,2008,512]{3,2,1,0:T(8,128)S(1)}, f32[1,1,2008,512]{3,2,1,0:T(8,128)}, u32[]{:S(2)}) copy-start(f32[1,1,2008,512]{3,2,1,0:T(8,128)} %param.17) | copy-start | bytes 12337156
  22.3 2.0 collective-permute-start.1
  22.4 57.7 %copy-start.12 = (f32[2,512]{1,0:T(2,128)S(1)}, f32[2,512]{1,0:T(2,128)}, u32[]{:S(2)}) copy-start(f32[2,512]{1,0:T(2,128)} %param.14) | copy-start | bytes 12292
  22.4 57.7 %copy-start.13 = (f32[2,512]{1,0:T(2,128)S(1)}, f32[2,512]{1,0:T(2,128)}, u32[]{:S(2)}) copy-start(f32[2,512]{1,0:T(2,128)} %param.15) | copy-start | bytes 12292
  22.4 57.7 %copy-start.14 = (bf16[1,4,512]{2,1,0:T(4,128)(2,1)S(1)}, bf16[1,4,512]{2,1,0:T(4,128)(2,1)}, u32[]{:S(2)}) copy-start(bf16[1,4,512]{2,1,0:T(4,128)(2,1)} %param.16) | copy-start | bytes 12292
  24.3 0.9 copy-start.8
  25.1 69.7 %collective-permute-start.3 = (f32[32,2008]{1,0:T(8,128)}, f32[32,2008]{1,0:T(8,128)}, u32[]{:S(2)}, u32[]{:S(2)}) collective-permute-start(f32[32,2008]{1,0:T(8,128)} %slice_bitcast_fusion), channel_id=1, source_target_pairs={{0,16},{16,0},{1,17},{17,1},{2,18},{18,2},{3,19},{19,3},{4,20},{20... | collective-permute-start | bytes 771080 | tf_op jit(solution)/shard_map/ppermute | solution.py:27
  80.0 2.3 copy-start.7
  81.5 9.1 %copy-start.11 = (f32[2,512]{1,0:T(2,128)}, f32[2,512]{1,0:T(2,128)S(1)}, u32[]{:S(2)}) copy-start(f32[2,512]{1,0:T(2,128)S(1)} %get-tuple-element.24) | copy-start | bytes 12292
  87.9 2.7 %copy-start.6 = (f32[2,12,128,512]{3,2,1,0:T(8,128)}, f32[2,12,128,512]{3,2,1,0:T(8,128)S(1)}, u32[]{:S(2)}) copy-start(f32[2,12,128,512]{3,2,1,0:T(8,128)S(1)} %get-tuple-element.26) | copy-start | bytes 18874372
  90.6 14.1 %copy-start.5 = (f32[12,128,512]{2,1,0:T(8,128)}, f32[12,128,512]{2,1,0:T(8,128)S(1)}, u32[]{:S(2)}) copy-start(f32[12,128,512]{2,1,0:T(8,128)S(1)} %get-tuple-element.27) | copy-start | bytes 9437188
  90.6 4.2 %copy-start.9 = (f32[2,32,2008]{2,1,0:T(8,128)S(1)}, f32[2,32,2008]{2,1,0:T(8,128)}, u32[]{:S(2)}) copy-start(f32[2,32,2008]{2,1,0:T(8,128)} %copy-done.8) | copy-start | bytes 1542148
  92.8 94.4 %collective-permute-start.2 = (f32[1538,512]{1,0:T(8,128)}, f32[1538,512]{1,0:T(8,128)}, u32[]{:S(2)}, u32[]{:S(2)}) collective-permute-start(f32[1538,512]{1,0:T(8,128)} %pad_maximum_fusion.1), channel_id=1, source_target_pairs={{0,16},{16,0},{1,17},{17,1},{2,18},{18,2},{3,19},{19,3},{4,20},{20... | collective-permute-start | bytes 9449480 | tf_op jit(solution)/shard_map/ppermute | solution.py:27
  96.5 1.9 collective-permute-start.4
  99.5 5.3 %copy-start.1 = (f32[1,1,2008,512]{3,2,1,0:T(8,128)S(1)}, f32[1,1,2008,512]{3,2,1,0:T(8,128)}, u32[]{:S(2)}) copy-start(f32[1,1,2008,512]{3,2,1,0:T(8,128)} %param.18) | copy-start | bytes 12337156
  99.5 6.4 %copy-start.4 = (f32[1,1,2008,512]{3,2,1,0:T(8,128)S(1)}, f32[1,1,2008,512]{3,2,1,0:T(8,128)}, u32[]{:S(2)}) copy-start(f32[1,1,2008,512]{3,2,1,0:T(8,128)} %param.17) | copy-start | bytes 12337156
  111.7 2.9 %copy-start.2 = (f32[2008,512]{1,0:T(8,128)}, f32[2008,512]{1,0:T(8,128)S(1)}, u32[]{:S(2)}) copy-start(f32[2008,512]{1,0:T(8,128)S(1)} %get-tuple-element.22) | copy-start | bytes 12337156
  111.8 74.4 %collective-permute-start.5 = (f32[496,512]{1,0:T(8,128)S(1)}, f32[496,512]{1,0:T(8,128)S(1)}, u32[]{:S(2)}, u32[]{:S(2)}) collective-permute-start(f32[496,512]{1,0:T(8,128)S(1)} %slice.53), channel_id=1, source_target_pairs={{0,16},{16,0},{1,17},{17,1},{2,18},{18,2},{3,19},{19,3},{4,20},{20... | collective-permute-start | bytes 3047432 | tf_op jit(solution)/shard_map/ppermute | solution.py:27
  114.6 93.7 %collective-permute-start.8 = (f32[504,512]{1,0:T(8,128)}, f32[504,512]{1,0:T(8,128)S(1)}, u32[]{:S(2)}, u32[]{:S(2)}) collective-permute-start(f32[504,512]{1,0:T(8,128)} %get-tuple-element.31), channel_id=1, source_target_pairs={{0,16},{16,0},{1,17},{17,1},{2,18},{18,2},{3,19},{19,3},{4,20},{20... | collective-permute-start | bytes 3096584 | tf_op jit(solution)/shard_map/ppermute | solution.py:27
  115.6 114.8 %collective-permute-start.7 = (f32[504,512]{1,0:T(8,128)}, f32[504,512]{1,0:T(8,128)S(1)}, u32[]{:S(2)}, u32[]{:S(2)}) collective-permute-start(f32[504,512]{1,0:T(8,128)} %get-tuple-element.32), channel_id=1, source_target_pairs={{0,16},{16,0},{1,17},{17,1},{2,18},{18,2},{3,19},{19,3},{4,20},{20... | collective-permute-start | bytes 3096584 | tf_op jit(solution)/shard_map/ppermute | solution.py:27
  116.7 133.2 %collective-permute-start.6 = (f32[504,512]{1,0:T(8,128)}, f32[504,512]{1,0:T(8,128)S(1)}, u32[]{:S(2)}, u32[]{:S(2)}) collective-permute-start(f32[504,512]{1,0:T(8,128)} %get-tuple-element.33), channel_id=1, source_target_pairs={{0,16},{16,0},{1,17},{17,1},{2,18},{18,2},{3,19},{19,3},{4,20},{20... | collective-permute-start | bytes 3096584 | tf_op jit(solution)/shard_map/ppermute | solution.py:27

commit v3 on v2

--- a/solution.py
+++ b/solution.py
@@ -6,7 +6,7 @@
 OUTER_RATE = 0.7
 MOMENTUM = 0.9
 SWAP = ((0, 1), (1, 0))
-EMB_CUTS = (0, 3, 6, 9, 12)
+EMB_CUTS = (0, 4, 8, 10, 11, 12)
 TWELFTHS = 12
 LOW = 256
 
@@ -86,19 +86,11 @@
     half_width = emb_global.shape[3]
     rank = basis.shape[1]
 
-    width = attn_global.shape[2]
-
-    def pack(attn, norm):
-        return jnp.concatenate((attn.reshape(-1, width), norm), axis=0)
-
-    def unpack(rows):
-        return rows[:-norm_owned].reshape(attn_global.shape), rows[-norm_owned:]
-
-    def mean_part(inner, owned, owner):
-        part = lax.dynamic_slice_in_dim(inner[0], owner * owned, owned, 0)
+    def mean_part(owner):
+        part = lax.dynamic_slice_in_dim(attn_inner[0], owner * attn_owned, attn_owned, 0)
         return part.astype(jnp.float32) / groups
 
-    leaving = pack(mean_part(attn_inner, attn_owned, other), mean_part(norm_inner, norm_owned, other))
+    leaving = mean_part(other)
     arrived = swap(leaving, "rep")
 
     touched = after(touched, leaving)
@@ -125,17 +117,22 @@
     kept = lax.dynamic_slice_in_dim(terms, tp_index * half_rank, half_rank, 1)
     given = lax.dynamic_slice_in_dim(terms, (1 - tp_index) * half_rank, half_rank, 1)
     summed = kept + swap(given, "tp")
-    coeff_arrived = swap(summed[1], "rep")
-
-    attn_arrived, norm_arrived = unpack(after(arrived, summed))
-    attn_mean = mean_part(attn_inner, attn_owned, rep_index) + attn_arrived
-    norm_mean = mean_part(norm_inner, norm_owned, rep_index) + norm_arrived
-    new_attn_global, new_attn_momentum = nesterov(attn_global, attn_momentum, attn_global - attn_mean)
-    new_norm_global, new_norm_momentum = nesterov(norm_global, norm_momentum, norm_global - norm_mean)
-    back = pack(new_attn_global, new_norm_global)
-    returned = swap(back, "rep")
-
-    coeff_mine = summed[0] + after(coeff_arrived, back)
+
+    norm_sent = jnp.concatenate((norm_inner[0].astype(jnp.float32) / groups, norm_global, norm_momentum), axis=0)
+    norm_lines = -(-norm_sent.size // half_rows)
+    norm_flat = jnp.pad(norm_sent.reshape(-1), (0, norm_lines * half_rows - norm_sent.size))
+    packed = jnp.concatenate((summed[1], norm_flat.reshape(norm_lines, half_rows)), axis=0)
+    packed_arrived = swap(packed, "rep")
+
+    attn_mean = mean_part(rep_index) + after(arrived, packed)
+    new_attn_global, _ = nesterov(attn_global, attn_momentum, attn_global - attn_mean)
+    returned = swap(new_attn_global, "rep")
+
+    packed_arrived = after(packed_arrived, new_attn_global)
+    coeff_arrived = packed_arrived[:half_rank]
+    norm_got = packed_arrived[half_rank:].reshape(-1)[: norm_sent.size].reshape(norm_sent.shape)
+
+    coeff_mine = summed[0] + coeff_arrived
     coeff_theirs = swap(coeff_mine, "tp")
     first = tp_index == 0
     coeff_sum = jnp.concatenate(
@@ -157,16 +154,30 @@
     )
     fresh_rows, fresh_momentum = nesterov(own_rows, own_momentum, emb_grad)
     emb_cuts = cuts(half_rows, EMB_CUTS, 8)
-    emb_returned = [swap(fresh_rows[a:b], "rep") for a, b in emb_cuts]
-
-    attn_returned, norm_returned = unpack(returned)
-    attn_weights = put(placed(new_attn_global, rep_index), attn_returned, 0, rep_index)
+    emb_weights = placed(fresh_rows, rep_index)
+    emb_returned = []
+    for i, (a, b) in enumerate(emb_cuts):
+        piece = fresh_rows[a:b]
+        if i >= 2:
+            emb_weights = put(emb_weights, emb_returned[i - 2], emb_cuts[i - 2][0], rep_index)
+            piece = after(piece, emb_weights)
+        emb_returned.append(swap(piece, "rep"))
+
+    late, late_own = after((arrived, new_attn_global), fresh_rows)
+    late_mean = mean_part(rep_index) + late
+    _, new_attn_momentum = nesterov(attn_global, attn_momentum, attn_global - late_mean)
+    attn_weights = put(placed(late_own, rep_index), returned, 0, rep_index)
+    inner_rows = norm_inner.shape[1]
+    norm_total = norm_sent[:inner_rows] + norm_got[:inner_rows]
+    norm_mean = lax.dynamic_slice_in_dim(norm_total, rep_index * norm_owned, norm_owned, 0)
+    new_norm_global, new_norm_momentum = nesterov(norm_global, norm_momentum, norm_global - norm_mean)
+    norm_theirs = norm_got[inner_rows : inner_rows + norm_owned]
+    norm_mean = lax.dynamic_slice_in_dim(norm_total, other * norm_owned, norm_owned, 0)
+    norm_returned, _ = nesterov(norm_theirs, norm_got[inner_rows + norm_owned :], norm_theirs - norm_mean)
     norm_weights = put(placed(new_norm_global, rep_index), norm_returned, 0, rep_index)
-    emb_weights = placed(fresh_rows, rep_index)
-    for i, ((a, _), got) in enumerate(zip(emb_cuts, emb_returned)):
-        if i >= 1:
-            got = after(got, (attn_weights, norm_weights))
-        emb_weights = put(emb_weights, got, a, rep_index)
+    done = (attn_weights, norm_weights, new_attn_momentum, new_norm_momentum)
+    for (a, _), got in list(zip(emb_cuts, emb_returned))[-2:]:
+        emb_weights = put(emb_weights, after(got, done), a, rep_index)
     attn_weights, norm_weights, emb_weights = [
         halves.reshape((-1,) + halves.shape[2:]) for halves in (attn_weights, norm_weights, emb_weights)
     ]

time: 253 us -> 243 us (0.960)
  waiting for transfers between devices: 179 us -> 163 us
  starting transfers between devices: 8.34 us -> 11.3 us
  other arithmetic: 19.9 us -> 22.7 us
    ppermute x9 -> x10, waiting for transfers between devices: 179 us -> 163 us  [swap(): return lax.ppermute(x, axis, SWAP)]
    dynamic_update_slice x2 -> x1, other arithmetic: 7.06 us -> 0.61 us  [placed(): lax.dynamic_update_slice(halves, own[None], (rep_index,) + (0,) * own.ndim)]
    sub x0 -> x1, other arithmetic: none -> 5.72 us  [nesterov(): global_part - OUTER_RATE * (outer_grad + MOMENTUM * fresh_momentum)]
    add x1 -> x3, other arithmetic: 1.69 us -> 5.88 us  [the longest x1 4.84 us: nesterov(): fresh_momentum = MOMENTUM * momentum_part + outer_grad]
    broadcast_in_dim x3, local copies, waits for them, and re-layouts: 6.02 us -> 1.83 us  [placed(): halves = jnp.zeros((2,) + own.shape, jnp.float32)]
    concatenate x2 -> x1, other arithmetic: 4.12 us -> 0.03 us  [per_device(): jnp.concatenate((summed[1], norm_flat.reshape(norm_lines, half_rows)), ax...]
    ppermute x9 -> x10, starting transfers between devices: 8.34 us -> 11.3 us  [swap(): return lax.ppermute(x, axis, SWAP)]
    unnamed x31 -> x36, local copies, waits for them, and re-layouts: 4.72 us -> 6.82 us
  transfers between devices with their start and end apart: 9 -> 10, of which waited for: 7 -> 8; matrix products, arithmetic and copies ran while one was open for 21% -> 22% of each run, Pallas kernels for 0% -> 0%
where the time goes in v3:
time: 243 us; the launch traced here: 242 us
  waiting for transfers between devices  163 us (67%)
  local copies, waits for them, and re-layouts  24.2 us (10%)
  other arithmetic  22.7 us (9%)
  matrix products  19.4 us (8%)
  starting transfers between devices  11.3 us (5%)
    ppermute x10, waiting for transfers between devices, swap(): return lax.ppermute(x, axis, SWAP)  163 us
    ppermute x10, starting transfers between devices, swap(): return lax.ppermute(x, axis, SWAP)  11.3 us
    dot_general x3, matrix products, coeff_of(): lax.dot_general(basis_half, rows, (((0,), (1,)), ((), ())), precision=lax...  10.7 us
    dynamic_update_slice x6, local copies, waits for them, and re-layouts, put(): lax.dynamic_update_slice(halves, piece[None], (1 - rep_index, at) + (0,)...  8.35 us
    unnamed x36, local copies, waits for them, and re-layouts  6.82 us
    dot_general x1, matrix products, per_device(): lax.dot_general(coeff_sum, basis_half, (((0,), (1,)), ((), ())), precisio...  6.04 us
    slice x4, local copies, waits for them, and re-layouts, per_device(): piece = fresh_rows[a:b]  5.77 us
    sub x1, other arithmetic, nesterov(): global_part - OUTER_RATE * (outer_grad + MOMENTUM * fresh_momentum)  5.72 us
  transfers between devices with their start and end apart: 10, of which 8 were waited for; matrix products, arithmetic and copies ran while one was open for 22% of the time, Pallas kernels for 0%

profile of v3, /device:TPU:0, one launch (start us, length us, event | category | flops | bytes accessed | tf_op | source)
XLA Modules:
  0.0 242.2 jit_solution(14733991859960524156)
XLA Ops:
  0.6 0.0 copy-start
  0.7 3.6 %multiply_bitcast_fusion = f32[12,128,512]{2,1,0:T(8,128)} fusion(bf16[1,24,128,512]{3,2,1,0:T(8,128)(2,1)} %param.13, s32[]{:T(128)S(6)} %select_n.67), kind=kLoop, calls=%fused_computation.17 | loop fusion | flops 1572864 | bytes 4718596 | tf_op jit(solution)/shard_map/div | solution.py:91
  4.2 3.0 %collective-permute-start = (f32[12,128,512]{2,1,0:T(8,128)}, f32[12,128,512]{2,1,0:T(8,128)}, u32[]{:S(2)}, u32[]{:S(2)}) collective-permute-start(f32[12,128,512]{2,1,0:T(8,128)} %multiply_bitcast_fusion), channel_id=1, source_target_pairs={{0,16},{16,0},{1,17},{17,1},{2,18},{18,2},{3,19},{19,3},{4,20},{20... | collective-permute-start | bytes 9437192 | tf_op jit(solution)/shard_map/ppermute | solution.py:27
  7.2 0.2 multiply_subtract_fusion.1
  7.4 2.7 %fusion.23 = pred[1,2,16,256]{3,2,1,0:T(8,128)(4,1)S(1)} fusion(s32[2,8192]{1,0:T(2,128)S(1)} %get-tuple-element.34, s32[2,8192]{1,0:T(2,128)S(1)} %get-tuple-element.35), kind=kOutput, calls=%fused_computation.36 | convolution fusion | flops 138682368 | bytes 139264 | tf_op jit(solution)/shard_map/rht,rlt->rhl/dot_general | solution.py:50
  10.1 0.1 reshape.87
  10.3 0.1 reduce_sum.12
  10.4 0.0 copy-start.5
  10.4 3.6 %fusion.17 = f32[1,64,2008]{2,1,0:T(8,128)S(1)} fusion(bf16[2,2008,512]{2,1,0:T(8,128)(2,1)} %bitcast.89, s32[]{:T(128)S(6)} %select_n.72, f32[2008]{0:T(1024)S(1)} %bitcast.96, f32[1024,64]{0,1:T(8,128)S(1)} %copy-done, s32[]{:T(128)S(6)} %select_n.70), kind=kOutput, calls=%fused_computation.24 | convolution fusion | flops 789706240 | bytes 2709512 | tf_op jit(solution)/shard_map/dot_general | solution.py:56
  14.0 3.4 %convolution_multiply_fusion.1 = f32[64,2008]{1,0:T(8,128)S(1)} fusion(bf16[2,2008,512]{2,1,0:T(8,128)(2,1)} %bitcast.90, s32[]{:T(128)S(6)} %select_n.69, f32[2008]{0:T(1024)S(1)} %bitcast.95, f32[1024,64]{0,1:T(8,128)S(1)} %copy-done, s32[]{:T(128)S(6)} %select_n.70), kind=kOutput, calls=%fused_computation.23 | convolution fusion | flops 789706240 | bytes 2709512 | tf_op jit(solution)/shard_map/dot_general | solution.py:56
  17.5 0.0 copy-start.14
  17.5 0.0 copy-start.15
  17.5 0.0 copy-start.16
  17.5 3.8 %fusion.14 = f32[1,64,2008]{2,1,0:T(8,128)S(1)} fusion(f32[64,2008]{1,0:T(8,128)S(1)} %convolution_multiply_fusion.1, f32[1,1,2008,512]{3,2,1,0:T(8,128)S(1)} %copy-done.5, f32[2008]{0:T(1024)S(1)} %bitcast.94, f32[1024,64]{0,1:T(8,128)S(1)} %copy-done, s32[]{:T(128)S(6)} %select_n.70), kind=kOutput, calls=%fused_computation.21 | convolution fusion | flops 789834752 | bytes 5289988 | tf_op jit(solution)/shard_map/dot_general | solution.py:56
  21.3 0.1 collective-permute-start.1
  21.5 0.1 reshape.89
  21.6 1.7 collective-permute-done.1
  23.3 0.1 fusion.26
  23.4 0.1 collective-permute-start.2
  23.5 53.0 %collective-permute-done = f32[12,128,512]{2,1,0:T(8,128)} collective-permute-done((f32[12,128,512]{2,1,0:T(8,128)}, f32[12,128,512]{2,1,0:T(8,128)}, u32[]{:S(2)}, u32[]{:S(2)}) %collective-permute-start) | collective-permute-done | bytes 3145760 | tf_op jit(solution)/shard_map/ppermute | solution.py:27
  76.4 5.7 %multiply_subtract_fusion = f32[12,128,512]{2,1,0:T(8,128)S(1)} fusion(f32[12,128,512]{2,1,0:T(8,128)} %param.11, f32[12,128,512]{2,1,0:T(8,128)} %collective-permute-done, f32[12,128,512]{2,1,0:T(8,128)} %param.12, bf16[1,24,128,512]{3,2,1,0:T(8,128)(2,1)} %param.13, s32[]{:T(128)S(6)} %select_n.66), kind=kLoop, calls=%fused_computation.16 | loop fusion | flops 7864320 | bytes 14155780 | tf_op jit(solution)/shard_map/sub | solution.py:16
  82.2 0.0 copy-start.7
  82.2 0.4 collective-permute-done.2
  82.5 1.0 fusion.32
  83.6 1.5 collective-permute-start.4
  85.1 0.0 collective-permute-start.3
  85.1 0.1 reshape.91
  85.3 0.6 constant_dynamic-update-slice_fusion.1
  85.9 1.1 collective-permute-done.3
  87.0 1.1 broadcast_select_fusion.1
  88.1 0.0 copy-start.2
  88.1 0.0 copy-start.6
  88.1 1.0 broadcast_in_dim.52
  89.1 1.1 copy-done.2
  90.2 1.3 copy-done.6
  91.5 6.0 %bitcast_dynamic-update-slice_fusion = (f32[2,2008,512]{2,1,0:T(8,128)S(1)}, f32[2008,512]{1,0:T(8,128)S(1)}, f32[2008,512]{1,0:T(8,128)}) fusion(f32[2,2008,512]{2,1,0:T(8,128)S(1)} %broadcast_in_dim.52, s32[]{:T(128)S(6)} %select_n.69, f32[1,1,2008,512]{3,2,1,0:T(8,128)S(1)} %copy-done.2, f32[1,1,2008,512]{3,2,1,0:T(8,128)S(1)} %copy-done.6, ...), kind=kOutput, calls=%fused_computation.3 | convolution fusion | flops 796902912 | bytes 21217288 | tf_op jit(solution)/shard_map/dot_general | solution.py:146
  97.5 2.0 copy-done.4
  99.5 1.8 slice.79
  101.3 1.4 copy-done.10
  102.6 0.5 collective-permute-start.5
  103.2 0.6 reshape.92
  103.8 1.3 slice.81
  105.1 1.6 slice.80
  106.7 1.6 collective-permute-start.6
  108.2 5.4 %fusion.4 = f32[1,1,2008,512]{3,2,1,0:T(8,128)} fusion(f32[2008,512]{1,0:T(8,128)} %get-tuple-element.44, f32[1,1,2008,512]{3,2,1,0:T(8,128)S(1)} %copy-done.3), kind=kLoop, calls=%fused_computation.8 | loop fusion | flops 3084288 | bytes 12337152 | tf_op jit(solution)/shard_map/reshape | solution.py:193
  113.7 1.0 copy-done.11
  114.7 4.8 %fusion.7 = f32[12,128,512]{2,1,0:T(8,128)} fusion(f32[12,128,512]{2,1,0:T(8,128)S(1)} %copy-done.8, f32[12,128,512]{2,1,0:T(8,128)} %collective-permute-done, f32[12,128,512]{2,1,0:T(8,128)S(1)} %copy-done.9, bf16[1,24,128,512]{3,2,1,0:T(8,128)(2,1)S(1)} %copy-done.11, s32[]{:T(128)S(6)} %select_n.66), kind=kLoop, calls=%fused_computation.15 | loop fusion | flops 4718592 | bytes 14155780 | tf_op jit(solution)/shard_map/add | solution.py:15
  119.6 64.3 %collective-permute-done.5 = f32[664,512]{1,0:T(8,128)} collective-permute-done((f32[664,512]{1,0:T(8,128)}, f32[664,512]{1,0:T(8,128)}, u32[]{:S(2)}, u32[]{:S(2)}) %collective-permute-start.5) | collective-permute-done | bytes 1359904 | tf_op jit(solution)/shard_map/ppermute | solution.py:27
  183.9 2.5 %bitcast_dynamic-update-slice_fusion.4 = f32[2,2008,512]{2,1,0:T(8,128)} fusion(f32[2,2008,512]{2,1,0:T(8,128)} %copy-done.10, s32[]{:T(128)S(6)} %select_n.72, f32[664,512]{1,0:T(8,128)} %collective-permute-done.5), kind=kLoop, calls=%fused_computation.30 | loop fusion | bytes 2719748 | tf_op jit(solution)/shard_map/dynamic_update_slice | solution.py:40
  186.4 1.5 collective-permute-start.7
  187.9 1.1 fusion.46
  189.0 0.8 broadcast_in_dim.46
  189.8 0.4 bitcast_dynamic-update-slice_fusion.2
  190.2 23.0 %collective-permute-done.6 = f32[672,512]{1,0:T(8,128)S(1)} collective-permute-done((f32[672,512]{1,0:T(8,128)S(1)}, f32[672,512]{1,0:T(8,128)S(1)}, u32[]{:S(2)}, u32[]{:S(2)}) %collective-permute-start.6) | collective-permute-done | bytes 1376288 | tf_op jit(solution)/shard_map/ppermute | solution.py:27
  213.3 1.2 bitcast_dynamic-update-slice_fusion.3
  214.4 1.5 collective-permute-start.8
  216.0 12.0 %collective-permute-done.7 = f32[336,512]{1,0:T(8,128)S(1)} collective-permute-done((f32[336,512]{1,0:T(8,128)S(1)}, f32[336,512]{1,0:T(8,128)S(1)}, u32[]{:S(2)}, u32[]{:S(2)}) %collective-permute-start.7) | collective-permute-done | bytes 688160 | tf_op jit(solution)/shard_map/ppermute | solution.py:27
  228.0 0.9 bitcast_dynamic-update-slice_fusion.5
  228.9 1.5 collective-permute-start.9
  230.4 2.3 bitcast_dynamic-update-slice_fusion.1
  232.7 0.0 copy-start.12
  232.7 8.0 %collective-permute-done.9 = f32[168,512]{1,0:T(8,128)S(1)} collective-permute-done((f32[168,512]{1,0:T(8,128)S(1)}, f32[168,512]{1,0:T(8,128)S(1)}, u32[]{:S(2)}, u32[]{:S(2)}) %collective-permute-start.9) | collective-permute-done | bytes 344096 | tf_op jit(solution)/shard_map/ppermute | solution.py:27
  240.7 0.8 bitcast_dynamic-update-slice_fusion.7
  241.4 0.8 bitcast_dynamic-update-slice_fusion.6
  (43 shorter events, 0.4 us)
Async XLA Ops:
  0.6 9.8 %copy-start = (f32[1024,64]{0,1:T(8,128)S(1)}, f32[1024,64]{0,1:T(8,128)}, u32[]{:S(2)}) copy-start(f32[1024,64]{0,1:T(8,128)} %param.20) | copy-start | bytes 786436
  0.7 6.5 %copy-start.13 = (s32[2,8192]{1,0:T(2,128)S(1)}, s32[2,8192]{1,0:T(2,128)}, u32[]{:S(2)}) copy-start(s32[2,8192]{1,0:T(2,128)} %param.21) | copy-start | bytes 196612
  4.2 72.2 %collective-permute-start = (f32[12,128,512]{2,1,0:T(8,128)}, f32[12,128,512]{2,1,0:T(8,128)}, u32[]{:S(2)}, u32[]{:S(2)}) collective-permute-start(f32[12,128,512]{2,1,0:T(8,128)} %multiply_bitcast_fusion), channel_id=1, source_target_pairs={{0,16},{16,0},{1,17},{17,1},{2,18},{18,2},{3,19},{19,3},{4,20},{20... | collective-permute-start | bytes 9437192 | tf_op jit(solution)/shard_map/ppermute | solution.py:27
  10.4 7.1 %copy-start.5 = (f32[1,1,2008,512]{3,2,1,0:T(8,128)S(1)}, f32[1,1,2008,512]{3,2,1,0:T(8,128)}, u32[]{:S(2)}) copy-start(f32[1,1,2008,512]{3,2,1,0:T(8,128)} %param.17) | copy-start | bytes 12337156
  17.5 3.9 %copy-start.14 = (bf16[1,4,512]{2,1,0:T(4,128)(2,1)S(1)}, bf16[1,4,512]{2,1,0:T(4,128)(2,1)}, u32[]{:S(2)}) copy-start(bf16[1,4,512]{2,1,0:T(4,128)(2,1)} %param.16) | copy-start | bytes 12292
  17.5 4.0 %copy-start.15 = (f32[2,512]{1,0:T(2,128)S(1)}, f32[2,512]{1,0:T(2,128)}, u32[]{:S(2)}) copy-start(f32[2,512]{1,0:T(2,128)} %param.14) | copy-start | bytes 12292
  17.5 4.0 %copy-start.16 = (f32[2,512]{1,0:T(2,128)S(1)}, f32[2,512]{1,0:T(2,128)}, u32[]{:S(2)}) copy-start(f32[2,512]{1,0:T(2,128)} %param.15) | copy-start | bytes 12292
  21.3 2.0 collective-permute-start.1
  23.4 59.1 %collective-permute-start.2 = (f32[35,2008]{1,0:T(8,128)S(1)}, f32[35,2008]{1,0:T(8,128)S(1)}, u32[]{:S(2)}, u32[]{:S(2)}) collective-permute-start(f32[35,2008]{1,0:T(8,128)S(1)} %pad_maximum_fusion), channel_id=1, source_target_pairs={{0,16},{16,0},{1,17},{17,1},{2,18},{18,2},{3,19},{19,3},{4,20},{20... | collective-permute-start | bytes 843368 | tf_op jit(solution)/shard_map/ppermute | solution.py:27
  82.2 107.7 %copy-start.7 = (f32[12,128,512]{2,1,0:T(8,128)}, f32[12,128,512]{2,1,0:T(8,128)S(1)}, u32[]{:S(2)}) copy-start(f32[12,128,512]{2,1,0:T(8,128)S(1)} %multiply_subtract_fusion) | copy-start | bytes 9437188
  83.6 146.8 %collective-permute-start.4 = (f32[12,128,512]{2,1,0:T(8,128)S(1)}, f32[12,128,512]{2,1,0:T(8,128)}, u32[]{:S(2)}, u32[]{:S(2)}) collective-permute-start(f32[12,128,512]{2,1,0:T(8,128)S(1)} %multiply_subtract_fusion), channel_id=1, source_target_pairs={{0,16},{16,0},{1,17},{17,1},{2,18},{18,2},{3,19},{19,3},{4,20},{20... | collective-permute-start | bytes 9437192 | tf_op jit(solution)/shard_map/ppermute | solution.py:27
  85.1 1.9 collective-permute-start.3
  88.1 2.2 copy-start.2
  88.1 3.4 %copy-start.6 = (f32[1,1,2008,512]{3,2,1,0:T(8,128)S(1)}, f32[1,1,2008,512]{3,2,1,0:T(8,128)}, u32[]{:S(2)}) copy-start(f32[1,1,2008,512]{3,2,1,0:T(8,128)} %param.17) | copy-start | bytes 12337156
  97.5 2.0 copy-start.4
  97.5 5.1 %copy-start.10 = (f32[2,2008,512]{2,1,0:T(8,128)}, f32[2,2008,512]{2,1,0:T(8,128)S(1)}, u32[]{:S(2)}) copy-start(f32[2,2008,512]{2,1,0:T(8,128)S(1)} %get-tuple-element.29) | copy-start | bytes 24674308
  102.6 81.2 %collective-permute-start.5 = (f32[664,512]{1,0:T(8,128)}, f32[664,512]{1,0:T(8,128)}, u32[]{:S(2)}, u32[]{:S(2)}) collective-permute-start(f32[664,512]{1,0:T(8,128)} %slice.79), channel_id=1, source_target_pairs={{0,16},{16,0},{1,17},{17,1},{2,18},{18,2},{3,19},{19,3},{4,20},{20... | collective-permute-start | bytes 4079624 | tf_op jit(solution)/shard_map/ppermute | solution.py:27
  103.8 4.5 %copy-start.3 = (f32[1,1,2008,512]{3,2,1,0:T(8,128)S(1)}, f32[1,1,2008,512]{3,2,1,0:T(8,128)}, u32[]{:S(2)}) copy-start(f32[1,1,2008,512]{3,2,1,0:T(8,128)} %param.18) | copy-start | bytes 12337156
  106.7 106.6 %collective-permute-start.6 = (f32[672,512]{1,0:T(8,128)S(1)}, f32[672,512]{1,0:T(8,128)S(1)}, u32[]{:S(2)}, u32[]{:S(2)}) collective-permute-start(f32[672,512]{1,0:T(8,128)S(1)} %slice.80), channel_id=1, source_target_pairs={{0,16},{16,0},{1,17},{17,1},{2,18},{18,2},{3,19},{19,3},{4,20},{20... | collective-permute-start | bytes 4128776 | tf_op jit(solution)/shard_map/ppermute | solution.py:27
  108.2 5.4 %copy-start.8 = (f32[12,128,512]{2,1,0:T(8,128)S(1)}, f32[12,128,512]{2,1,0:T(8,128)}, u32[]{:S(2)}) copy-start(f32[12,128,512]{2,1,0:T(8,128)} %param.11) | copy-start | bytes 9437188
  108.2 5.4 %copy-start.9 = (f32[12,128,512]{2,1,0:T(8,128)S(1)}, f32[12,128,512]{2,1,0:T(8,128)}, u32[]{:S(2)}) copy-start(f32[12,128,512]{2,1,0:T(8,128)} %param.12) | copy-start | bytes 9437188
  108.2 6.5 %copy-start.11 = (bf16[1,24,128,512]{3,2,1,0:T(8,128)(2,1)S(1)}, bf16[1,24,128,512]{3,2,1,0:T(8,128)(2,1)}, u32[]{:S(2)}) copy-start(bf16[1,24,128,512]{3,2,1,0:T(8,128)(2,1)} %param.13) | copy-start | bytes 9437188
  186.4 41.6 %collective-permute-start.7 = (f32[336,512]{1,0:T(8,128)S(1)}, f32[336,512]{1,0:T(8,128)S(1)}, u32[]{:S(2)}, u32[]{:S(2)}) collective-permute-start(f32[336,512]{1,0:T(8,128)S(1)} %slice.81), channel_id=1, source_target_pairs={{0,16},{16,0},{1,17},{17,1},{2,18},{18,2},{3,19},{19,3},{4,20},{20... | collective-permute-start | bytes 2064392 | tf_op jit(solution)/shard_map/ppermute | solution.py:27
  214.4 26.3 %collective-permute-start.8 = (f32[168,512]{1,0:T(8,128)S(1)}, f32[168,512]{1,0:T(8,128)S(1)}, u32[]{:S(2)}, u32[]{:S(2)}) collective-permute-start(f32[168,512]{1,0:T(8,128)S(1)} %get-tuple-element.25), channel_id=1, source_target_pairs={{0,16},{16,0},{1,17},{17,1},{2,18},{18,2},{3,19},{19,3},{4,20},{20... | collective-permute-start | bytes 1032200 | tf_op jit(solution)/shard_map/ppermute | solution.py:27
  228.0 14.2 %copy-start.1 = (f32[1024,64]{0,1:T(8,128)S(1)}, f32[1024,64]{0,1:T(8,128)}, u32[]{:S(2)}) copy-start(f32[1024,64]{0,1:T(8,128)} %param.20) | copy-start | bytes 786436
  228.9 11.8 %collective-permute-start.9 = (f32[168,512]{1,0:T(8,128)S(1)}, f32[168,512]{1,0:T(8,128)S(1)}, u32[]{:S(2)}, u32[]{:S(2)}) collective-permute-start(f32[168,512]{1,0:T(8,128)S(1)} %get-tuple-element.27), channel_id=1, source_target_pairs={{0,16},{16,0},{1,17},{17,1},{2,18},{18,2},{3,19},{19,3},{4,20},{20... | collective-permute-start | bytes 1032200 | tf_op jit(solution)/shard_map/ppermute | solution.py:27
  232.7 9.5 %copy-start.12 = (f32[2,12,128,512]{3,2,1,0:T(8,128)}, f32[2,12,128,512]{3,2,1,0:T(8,128)S(1)}, u32[]{:S(2)}) copy-start(f32[2,12,128,512]{3,2,1,0:T(8,128)S(1)} %bitcast_dynamic-update-slice_fusion.1) | copy-start | bytes 18874372
